TPU v7x, 128 devices: a whole 4x4x4 slice. The times are simulated.
128 devices in a mesh: island: 4 (over y_hi, core), fsdp: 32 (over x, y_lo, z).
Axes of the slice: x: 4, y: 4 (y_hi: 2, y_lo: 2; y = y_hi * 2 + y_lo), z: 4, core: 2. Of those that a mesh axis runs over, the one named last changes fastest.
Arguments:
- tokens: bfloat16 [4, 16384, 8192], P('island', 'fsdp'), may hold values from -6 to 6
- cotangent: bfloat16 [4, 16384, 512], P('island', 'fsdp'), may hold values from -6 to 6
- weight: bfloat16 [4, 8192, 512], P('island', 'fsdp'), may hold values from -6 to 6
- moment_one: float32 [4, 8192, 512], P('island', 'fsdp'), may hold values from -4 to 4
- moment_two: float32 [4, 8192, 512], P('island', 'fsdp'), may hold values from 0.1 to 2
- step_count: int32 [4], P('island'), may hold values from 1 to 5, as said below
- outer_grad: float32 [4, 8192, 512], P('island', 'fsdp'), may hold values from -3 to 3
- outer_params: float32 [8192, 512], P('fsdp'), may hold values from -6 to 6
- outer_moment: float32 [8192, 512], P('fsdp'), may hold values from -3 to 3
Outputs:
- new_weight: bfloat16 [4, 8192, 512], P('island', 'fsdp')
- new_moment_one: float32 [4, 8192, 512], P('island', 'fsdp')
- new_moment_two: float32 [4, 8192, 512], P('island', 'fsdp')
- input_grad: bfloat16 [4, 16384, 8192], P('island', 'fsdp')
- new_outer_params: float32 [8192, 512], P('fsdp')
- new_outer_moment: float32 [8192, 512], P('fsdp')
Inputs may be any that keep to these rules, and one draw needn't show every extreme that they name: `step_count`: some island's counter is 5 and another island's counter is 1; the others may take any value in the range, equal or not.
All inputs are finite; a program needn't handle non-finite values.
Results may differ from a plain program's by a relative error of at most 0.015.
Values may be sent and summed in bfloat16 or wider, within the bound.
No kernel may reach another device: no remote copies, remote signals or barrier semaphores. Data moves between devices by JAX's collectives and lax.ppermute only.
A program may use at most 192 MiB of HBM per device.

v0:
```python
import math

import jax
import jax.numpy as jnp
from jax import lax
from jax.sharding import PartitionSpec as P

D = 8192


def outer_update(outer_grad, outer_params, outer_moment):
    count = lax.axis_size("island")
    delta = lax.psum(outer_grad[0].astype(jnp.bfloat16), "island").astype(jnp.float32) / count
    new_moment = 0.9 * outer_moment + delta
    new_params = outer_params - 0.7 * (delta + 0.9 * new_moment)
    return (new_params, new_moment)


def local(
    tokens,
    cotangent,
    weight,
    moment_one,
    moment_two,
    step_count,
    outer_grad,
    outer_params,
    outer_moment,
):
    scale = 1.0 / math.sqrt(D)
    new_params, new_moment = outer_update(outer_grad, outer_params, outer_moment)
    tok = tokens[0]
    cot = cotangent[0]
    wgt = weight[0]
    xf = tok.astype(jnp.float32)
    inv_rms = lax.rsqrt(jnp.mean(xf * xf, axis=-1, keepdims=True) + 1e-05)
    normed = xf * inv_rms
    hidden = normed.astype(jnp.bfloat16)
    prod = jnp.einsum(
        "tk,dk->td",
        cot,
        lax.all_gather(wgt, "fsdp", axis=0, tiled=True),
        preferred_element_type=jnp.float32,
    )
    grad_h = (prod * scale).astype(jnp.bfloat16)
    grad = lax.psum_scatter(
        (jnp.einsum("td,tk->dk", hidden, cot, preferred_element_type=jnp.float32) * scale).astype(
            jnp.bfloat16
        ),
        "fsdp",
        scatter_dimension=0,
        tiled=True,
    ).astype(jnp.float32)
    grad_hf = grad_h.astype(jnp.float32)
    input_grad = (
        inv_rms * (grad_hf - normed * jnp.mean(grad_hf * normed, axis=-1, keepdims=True))
    ).astype(jnp.bfloat16)
    t_float = step_count[0].astype(jnp.float32)
    new_one = 0.9 * moment_one[0] + 0.1 * grad
    new_two = 0.95 * moment_two[0] + 0.05 * grad * grad
    corr_one = 1.0 - jnp.power(jnp.float32(0.9), t_float)
    corr_two = 1.0 - jnp.power(jnp.float32(0.95), t_float)
    update = new_one / corr_one / (jnp.sqrt(new_two / corr_two) + 1e-08)
    wf = wgt.astype(jnp.float32)
    new_w = (wf - 0.15 * (update + 0.1 * wf)).astype(jnp.bfloat16)
    return (new_w[None], new_one[None], new_two[None], input_grad[None], new_params, new_moment)


def solution(mesh):
    placed = (
        P("island", "fsdp", None),
        P("island", "fsdp", None),
        P("island", "fsdp", None),
        P("island", "fsdp", None),
        P("island", "fsdp", None),
        P("island"),
        P("island", "fsdp", None),
        P("fsdp", None),
        P("fsdp", None),
    )
    return jax.shard_map(
        local,
        mesh=mesh,
        in_specs=placed,
        out_specs=(
            P("island", "fsdp", None),
            P("island", "fsdp", None),
            P("island", "fsdp", None),
            P("island", "fsdp", None),
            P("fsdp", None),
            P("fsdp", None),
        ),
        check_vma=False,
    )
```

profile of v0, /device:TPU:0, one launch (start us, length us, event | category | flops | bytes accessed | tf_op | source)
XLA Modules:
  0.0 375.0 jit_solution(1393758994445669090)
XLA Ops:
  8.0 0.0 copy-start
  8.0 0.0 all-reduce.2.cloned.1.call-start
  8.1 1.8 convert_bitcast_fusion.1
  9.9 0.0 all-reduce.2.cloned.1.call-update
  9.9 0.0 all-gather.3.cloned.1.call-start
  10.0 0.5 all-gather.3.cloned.1.call-update
  10.5 0.0 reduce-scatter.2.cloned.1.call-start
  10.5 0.0 copy-start.1
  10.5 5.3 %fusion.3 = f32[512]{0:T(512)S(1)} fusion(bf16[1,512,8192]{2,1,0:T(8,128)(2,1)} %param.9), kind=kLoop, calls=%fused_computation.7 | loop fusion | flops 12582400 | bytes 8390656 | tf_op jit(solution)/shard_map/reduce_sum | solution.py:36
  15.8 0.0 copy-done
  15.8 0.5 copy-done.1
  16.3 7.0 %multiply_convert_fusion.1 = bf16[8192,512]{1,0:T(8,128)(2,1)} fusion(bf16[1,512,8192]{2,1,0:T(8,128)(2,1)S(1)} %copy-done.1, f32[512]{0:T(512)S(1)} %add_rsqrt_fusion, bf16[1,512,512]{2,1,0:T(8,128)(2,1)S(1)} %copy-done), kind=kOutput, calls=%fused_computation.13 | convolution fusion | flops 4315938816 | bytes 17303552 | tf_op jit(solution)/shard_map/td,tk->dk/dot_general | solution.py:47
  23.3 0.0 copy-start.3
  23.3 0.0 copy-start.4
  23.3 0.0 reduce-scatter.2.cloned.1.call-update
  24.1 48.6 %all-reduce.2.cloned.1.call-done = bf16[256,512]{1,0:T(8,128)(2,1)} async-done(((bf16[256,512]{1,0:T(8,128)(2,1)}), bf16[256,512]{1,0:T(8,128)(2,1)}) %all-reduce.2.cloned.1.call-update) | async-done | bytes 262160 | tf_op jit(solution)/shard_map/psum | solution.py:13
  72.7 0.0 copy-done.3
  72.7 0.0 copy-done.4
  72.7 2.1 multiply_subtract_fusion
  74.8 108.0 %all-gather.3.cloned.1.call-done = bf16[1,8192,512]{2,1,0:T(8,128)(2,1)} async-done(((bf16[1,256,512]{2,1,0:T(8,128)(2,1)}), bf16[1,8192,512]{2,1,0:T(8,128)(2,1)}) %all-gather.3.cloned.1.call-update) | async-done | bytes 8388624 | tf_op jit(solution)/shard_map/all_gather | solution.py:42
  182.8 9.7 %fusion.5 = (f32[512]{0:T(512)S(1)}, bf16[512,8192]{1,0:T(8,128)(2,1)S(1)}) fusion(bf16[1,512,8192]{2,1,0:T(8,128)(2,1)} %param.9, f32[512]{0:T(512)S(1)} %add_rsqrt_fusion, bf16[1,8192,512]{2,1,0:T(8,128)(2,1)} %all-gather.3.cloned.1.call-done, bf16[1,512,512]{2,1,0:T(8,128)(2,1)S(1)} %copy-done), kind=kOutput, calls=%fused_computation.9 | convolution fusion | flops 4324326912 | bytes 25694208 | tf_op jit(solution)/shard_map/tk,dk->td/dot_general | solution.py:39
  192.5 0.0 copy-start.2
  192.6 0.0 copy-start.5
  192.6 0.0 copy-start.6
  192.6 9.2 %fusion.8 = bf16[1,512,8192]{2,1,0:T(8,128)(2,1)} fusion(bf16[1,512,8192]{2,1,0:T(8,128)(2,1)} %param.9, bf16[512,8192]{1,0:T(8,128)(2,1)S(1)} %get-tuple-element.12, f32[512]{0:T(512)S(1)} %broadcast_multiply_fusion, f32[512]{0:T(512)S(1)} %add_rsqrt_fusion), kind=kLoop, calls=%fused_computation.14 | loop fusion | flops 29360128 | bytes 25169920 | tf_op jit(solution)/shard_map/broadcast_in_dim | solution.py:66
  201.8 163.4 %reduce-scatter.2.cloned.1.call-done = bf16[256,512]{1,0:T(8,128)(2,1)} async-done(((bf16[8192,512]{1,0:T(8,128)(2,1)}), bf16[256,512]{1,0:T(8,128)(2,1)}) %reduce-scatter.2.cloned.1.call-update) | async-done | bytes 262160 | tf_op jit(solution)/shard_map/reduce_scatter | solution.py:46
  365.1 0.0 copy-done.2
  365.1 0.0 copy-done.5
  365.1 0.0 copy-done.6
  365.1 2.4 fusion.21
  (2 shorter events, 0.0 us)
Async XLA Ops:
  8.0 7.8 %copy-start = (bf16[1,512,512]{2,1,0:T(8,128)(2,1)S(1)}, bf16[1,512,512]{2,1,0:T(8,128)(2,1)}, u32[]{:S(2)}) copy-start(bf16[1,512,512]{2,1,0:T(8,128)(2,1)} %param.10) | copy-start | bytes 1572868
  8.0 64.7 %all-reduce.2.cloned.1.call-start = ((), (), s32[]{:S(2)}) async-start(), calls=%async_computation.2 | async-start | bytes 524288 | tf_op jit(solution)/shard_map/psum | solution.py:13
  9.9 172.9 %all-gather.3.cloned.1.call-start = ((), (), s32[]{:S(2)}) async-start(), calls=%async_computation.3 | async-start | bytes 8650752 | tf_op jit(solution)/shard_map/all_gather | solution.py:42
  10.5 354.7 %reduce-scatter.2.cloned.1.call-start = ((), (), s32[]{:S(2)}) async-start(), calls=%async_computation.1 | async-start | bytes 8650752 | tf_op jit(solution)/shard_map/reduce_scatter | solution.py:46
  10.5 5.8 %copy-start.1 = (bf16[1,512,8192]{2,1,0:T(8,128)(2,1)S(1)}, bf16[1,512,8192]{2,1,0:T(8,128)(2,1)}, u32[]{:S(2)}) copy-start(bf16[1,512,8192]{2,1,0:T(8,128)(2,1)} %param.9) | copy-start | bytes 25165828
  23.3 49.4 %copy-start.3 = (f32[256,512]{1,0:T(8,128)S(1)}, f32[256,512]{1,0:T(8,128)}, u32[]{:S(2)}) copy-start(f32[256,512]{1,0:T(8,128)} %param.16) | copy-start | bytes 1572868
  23.3 49.5 %copy-start.4 = (f32[256,512]{1,0:T(8,128)S(1)}, f32[256,512]{1,0:T(8,128)}, u32[]{:S(2)}) copy-start(f32[256,512]{1,0:T(8,128)} %param.17) | copy-start | bytes 1572868
  192.5 172.6 %copy-start.2 = (bf16[1,256,512]{2,1,0:T(8,128)(2,1)S(1)}, bf16[1,256,512]{2,1,0:T(8,128)(2,1)}, u32[]{:S(2)}) copy-start(bf16[1,256,512]{2,1,0:T(8,128)(2,1)} %param.11) | copy-start | bytes 786436
  192.6 172.6 %copy-start.5 = (f32[1,256,512]{2,1,0:T(8,128)S(1)}, f32[1,256,512]{2,1,0:T(8,128)}, u32[]{:S(2)}) copy-start(f32[1,256,512]{2,1,0:T(8,128)} %param.13) | copy-start | bytes 1572868
  192.6 172.6 %copy-start.6 = (f32[1,256,512]{2,1,0:T(8,128)S(1)}, f32[1,256,512]{2,1,0:T(8,128)}, u32[]{:S(2)}) copy-start(f32[1,256,512]{2,1,0:T(8,128)} %param.12) | copy-start | bytes 1572868
Sparse Core Ops, SparseCore 0:
  11.9 60.7 all-reduce.1
Sparse Core Ops, SparseCore 1:
  12.0 170.7 all-gather.2
  185.1 180.0 reduce-scatter.1
where the time goes:
time: 375 us
  waiting for transfers between devices  320 us (85%)
  other arithmetic  20.8 us (6%)
  matrix products  16.7 us (4%)
  between operations  16.4 us (4%)
    reduce_scatter x1, waiting for transfers between devices, local(): lax.psum_scatter((jnp.einsum('td,tk->dk', hidden, cot, preferred_element_...  163 us
    all_gather x1, waiting for transfers between devices, local(): lax.all_gather(wgt, 'fsdp', axis=0, tiled=True)  108 us
    psum x1, waiting for transfers between devices, outer_update(): lax.psum(outer_grad[0].astype(jnp.bfloat16), 'island').astype(jnp.float32)  48.6 us
    dot_general x1, matrix products, local(): jnp.einsum('tk,dk->td', cot, lax.all_gather(wgt, 'fsdp', axis=0, tiled=Tr...  9.74 us
    broadcast_in_dim x1, other arithmetic, local(): input_grad[None]  9.19 us
  transfers between devices with their start and end apart: 3, of which 3 were waited for; matrix products, arithmetic and copies ran while one was open for 9% of the time, Pallas kernels for 0%

commit v1 on v0

v1 whole, which is shorter than its diff:
```python
import functools
import math

import jax
import jax.numpy as jnp
from jax import lax
from jax.experimental import pallas as pl
from jax.experimental.pallas import tpu as pltpu
from jax.sharding import PartitionSpec as P

D = 8192
KV = 512
TOK = 512
NX, NY, NZ = 4, 2, 4
LANE = 128
HALF = 4 * LANE
SCALE = 1.0 / math.sqrt(D)
MIB = 1 << 20

HBM = pl.BlockSpec(memory_space=pl.ANY)
VMEM = pl.BlockSpec(memory_space=pltpu.VMEM)
SMEM = pl.BlockSpec(memory_space=pltpu.SMEM)


def in_hbm(a):
    return pltpu.with_memory_space_constraint(a, pltpu.HBM)


def place(x, y, z):
    return ((x % NX) * NY + y % NY) * NZ + z % NZ


def shift(a, dx, dy, dz):
    pairs = [
        (place(x, y, z), place(x + dx, y + dy, z + dz))
        for x in range(NX)
        for y in range(NY)
        for z in range(NZ)
    ]
    return lax.ppermute(a, "fsdp", pairs)


GROUP_A = [[place(x, y, z) for y in range(NY) for z in range(NZ)] for x in range(NX)]


def column(pos_ref, part, far, dy, near):
    x, y, z = pos_ref[0], pos_ref[1], pos_ref[2]
    if part == 0:
        block = (((x + far) & 3) * NY + dy) * NZ + near
    else:
        block = (((x + near) & 3) * NY + ((y + dy) & 1)) * NZ + ((z + far) & 3)
    return pl.ds(pl.multiple_of((block * 2 + part) * LANE, LANE), LANE)


CHUNK = 128


def stats_kernel(tok_ref, cot_ref, tokv_ref, inv_ref, cots_ref, sem):
    copies = [
        pltpu.make_async_copy(
            tok_ref.at[pl.ds(i * CHUNK, CHUNK)], tokv_ref.at[pl.ds(i * CHUNK, CHUNK)], sem.at[i]
        )
        for i in range(TOK // CHUNK)
    ]
    for c in copies:
        c.start()
    for i in range(TOK // CHUNK):
        copies[i].wait()

        def rows_of(r, carry, i=i):
            rows = pl.ds(pl.multiple_of(i * CHUNK + r * 64, 64), 64)
            acc = jnp.zeros((64, LANE), jnp.float32)
            for j in range(D // LANE):
                t = tokv_ref[rows, j * LANE : (j + 1) * LANE].astype(jnp.float32)
                acc = acc + t * t
            inv = lax.rsqrt(jnp.sum(acc, axis=-1, keepdims=True) * (1.0 / D) + 1e-05)
            inv_ref[rows, :] = jnp.broadcast_to(inv, (64, LANE))
            cots_ref[rows, :] = (cot_ref[rows, :].astype(jnp.float32) * (inv * SCALE)).astype(
                jnp.bfloat16
            )
            return carry

        lax.fori_loop(0, CHUNK // 64, rows_of, 0)


def stats(tok, cot):
    return pl.pallas_call(
        stats_kernel,
        in_specs=[pl.BlockSpec(memory_space=pltpu.HBM), VMEM],
        out_specs=[VMEM, VMEM, VMEM],
        out_shape=[
            pltpu.VMEM((TOK, D), jnp.bfloat16),
            jax.ShapeDtypeStruct((TOK, LANE), jnp.float32),
            jax.ShapeDtypeStruct((TOK, KV), jnp.bfloat16),
        ],
        scratch_shapes=[pltpu.SemaphoreType.DMA((TOK // CHUNK,))],
        compiler_params=pltpu.CompilerParams(vmem_limit_bytes=16 * MIB),
        cost_estimate=pl.CostEstimate(flops=3 * TOK * D, bytes_accessed=10 * MIB, transcendentals=TOK),
        name="token_stats",
    )(tok, cot)


def grad_kernel(parts, pos_ref, tokv_ref, cots_ref, *outs):
    cots = cots_ref[...]
    for (part, far, dy), out in zip(parts, outs, strict=True):
        a = jnp.concatenate(
            [tokv_ref[:, column(pos_ref, part, far, dy, near)] for near in range(4)], axis=1
        )
        out[...] = lax.dot_general(
            a, cots, (((0,), (0,)), ((), ())), preferred_element_type=jnp.float32
        ).astype(jnp.bfloat16)


def grad_terms(pos, tokv, cots, parts, name):
    n = len(parts)
    return pl.pallas_call(
        functools.partial(grad_kernel, parts),
        in_specs=[SMEM, VMEM, VMEM],
        out_specs=[VMEM] * n,
        out_shape=[jax.ShapeDtypeStruct((HALF, KV), jnp.bfloat16)] * n,
        compiler_params=pltpu.CompilerParams(vmem_limit_bytes=16 * MIB),
        cost_estimate=pl.CostEstimate(
            flops=2 * TOK * KV * HALF * n, bytes_accessed=MIB * n, transcendentals=0
        ),
        name=name,
    )(pos, tokv, cots)


def product(pos_ref, cot_ref, tokv_ref, w, which, store, total):
    prod = lax.dot_general(
        cot_ref[...], w, (((1,), (1,)), ((), ())), preferred_element_type=jnp.float32
    )
    for near in range(4):
        p = prod[:, near * LANE : (near + 1) * LANE]
        store(near, p.astype(jnp.bfloat16))
        total = total + p * tokv_ref[:, column(pos_ref, *which, near)].astype(jnp.float32)
    return total


def gradh_kernel(parts, n_pieces, pos_ref, cot_ref, tokv_ref, *rest):
    pieces = rest[:n_pieces]
    gh_ref, acc_ref, wbuf, sem = rest[n_pieces:]
    copies, at = [], 0
    for k, piece in enumerate(pieces):
        rows = piece.shape[0]
        copies.append(pltpu.make_async_copy(piece, wbuf.at[pl.ds(at, rows)], sem.at[k]))
        copies[-1].start()
        at += rows
    loaded = 0
    for i, which in enumerate(parts):
        while loaded < n_pieces and sum(p.shape[0] for p in pieces[:loaded]) <= i * HALF:
            copies[loaded].wait()
            loaded += 1

        def store(near, p, i=i):
            at = (i * 4 + near) * LANE
            gh_ref[:, at : at + LANE] = p

        total = jnp.zeros((TOK, LANE), jnp.float32) if i == 0 else acc_ref[...]
        w = wbuf[i * HALF : (i + 1) * HALF, :]
        acc_ref[...] = product(pos_ref, cot_ref, tokv_ref, w, which, store, total)


def gradh(pos, cot, tokv, parts, pieces, name):
    n = len(parts)
    return pl.pallas_call(
        functools.partial(gradh_kernel, parts, len(pieces)),
        in_specs=[SMEM, VMEM, VMEM] + [HBM] * len(pieces),
        out_specs=[VMEM, VMEM],
        out_shape=[
            jax.ShapeDtypeStruct((TOK, HALF * n), jnp.bfloat16),
            jax.ShapeDtypeStruct((TOK, LANE), jnp.float32),
        ],
        scratch_shapes=[
            pltpu.VMEM((HALF * n, KV), jnp.bfloat16),
            pltpu.SemaphoreType.DMA((len(pieces),)),
        ],
        compiler_params=pltpu.CompilerParams(vmem_limit_bytes=20 * MIB),
        cost_estimate=pl.CostEstimate(
            flops=2 * TOK * KV * HALF * n, bytes_accessed=MIB * n, transcendentals=0
        ),
        name=name,
    )(pos, cot, tokv, *[in_hbm(p) for p in pieces])


TILE = 64


def input_kernel(parts, last, n_acc, pos_ref, inv_ref, cot_ref, tokv_ref, *rest):
    accs, ghs = rest[:n_acc], rest[n_acc : 2 * n_acc]
    pieces = rest[2 * n_acc : 2 * n_acc + len(last)]
    out_ref, outv, ghv, acc, wbuf, sem_in, sem_out = rest[2 * n_acc + len(last) :]
    copies = [pltpu.make_async_copy(p, wbuf.at[k], sem_in.at[k]) for k, p in enumerate(pieces)]
    for copy in copies:
        copy.start()
    total = accs[0][...]
    for a in accs[1:]:
        total = total + a[...]
    acc[...] = total
    for i, which in enumerate(last):

        def store(near, p, i=i):
            at = (i * 4 + near) * LANE
            ghv[:, at : at + LANE] = p

        copies[i].wait()
        acc[...] = product(pos_ref, cot_ref, tokv_ref, wbuf[i], which, store, acc[...])
    sources = []
    for g, group in zip((*ghs, ghv), (*parts, last), strict=True):
        for i, which in enumerate(group):
            sources += [(g, i * 4 + near, (*which, near)) for near in range(4)]

    def copy_of(tile):
        slot = lax.rem(tile, 2)
        return pltpu.make_async_copy(
            outv.at[slot], out_ref.at[pl.ds(pl.multiple_of(tile * TILE, TILE), TILE)], sem_out.at[slot]
        )

    def emit(tile, carry):
        rows = pl.ds(pl.multiple_of(tile * TILE, TILE), TILE)
        slot = lax.rem(tile, 2)

        @pl.when(tile >= 2)
        def _():
            copy_of(tile - 2).wait()

        inv = inv_ref[rows, :]
        total = jnp.sum(acc[rows, :], axis=-1, keepdims=True)
        first = inv * SCALE
        second = inv * inv * inv * (total * (SCALE / D))
        for g, at, where in sources:
            col = column(pos_ref, *where)
            gh = g[rows, at * LANE : (at + 1) * LANE].astype(jnp.float32)
            t = tokv_ref[rows, col].astype(jnp.float32)
            outv[slot, :, col] = (first * gh - second * t).astype(jnp.bfloat16)
        copy_of(tile).start()
        return carry

    tiles = TOK // TILE
    lax.fori_loop(0, tiles, emit, 0)
    copy_of(jnp.int32(tiles - 2)).wait()
    copy_of(jnp.int32(tiles - 1)).wait()


def input_gradient(pos, inv, cot, tokv, accs, ghs, parts, last, pieces):
    return pl.pallas_call(
        functools.partial(input_kernel, parts, last, len(accs)),
        in_specs=[SMEM] + [VMEM] * (3 + 2 * len(accs)) + [HBM] * len(last),
        out_specs=HBM,
        out_shape=jax.ShapeDtypeStruct((TOK, D), jnp.bfloat16),
        scratch_shapes=[
            pltpu.VMEM((2, TILE, D), jnp.bfloat16),
            pltpu.VMEM((TOK, HALF * len(last)), jnp.bfloat16),
            pltpu.VMEM((TOK, LANE), jnp.float32),
            pltpu.VMEM((len(last), HALF, KV), jnp.bfloat16),
            pltpu.SemaphoreType.DMA((len(last),)),
            pltpu.SemaphoreType.DMA((2,)),
        ],
        compiler_params=pltpu.CompilerParams(vmem_limit_bytes=20 * MIB),
        cost_estimate=pl.CostEstimate(
            flops=TOK * KV * D, bytes_accessed=24 * MIB, transcendentals=0
        ),
        name="input_gradient",
    )(pos, inv, cot, tokv, *accs, *ghs, *[in_hbm(p) for p in pieces])


def sum_kernel(plan, n_in, *refs):
    outs = refs[n_in:]
    for k, runs in enumerate(plan):
        row = 0
        for rows, members in runs:
            total = None
            for ref, at in members:
                v = refs[ref][at : at + rows, :]
                v = v.astype(jnp.float32) if len(members) > 1 else v
                total = v if total is None else total + v
            outs[k][row : row + rows, :] = total.astype(jnp.bfloat16)
            row += rows


def sums(*outs):
    arrays, plan, sizes = [], [], []
    for runs in outs:
        plan.append([])
        for rows, members in runs:
            where = []
            for a, at in members:
                if not any(a is b for b in arrays):
                    arrays.append(a)
                where.append(([a is b for b in arrays].index(True), at))
            plan[-1].append((rows, where))
        sizes.append(sum(rows for rows, _ in runs))
    r = pl.pallas_call(
        functools.partial(sum_kernel, plan, len(arrays)),
        in_specs=[VMEM] * len(arrays),
        out_specs=[VMEM] * len(outs),
        out_shape=[jax.ShapeDtypeStruct((n, KV), jnp.bfloat16) for n in sizes],
        compiler_params=pltpu.CompilerParams(vmem_limit_bytes=8 * MIB),
        cost_estimate=pl.CostEstimate(
            flops=sum(sizes) * KV, bytes_accessed=MIB * len(arrays), transcendentals=0
        ),
        name="sum_terms",
    )(*arrays)
    return r[0] if len(outs) == 1 else r


def after(value, *others):
    return lax.optimization_barrier((value, *others))[0]


class Queue:
    def __init__(self, depth):
        self.depth, self.got = depth, []

    def turn(self, a):
        return after(a, self.got[-self.depth]) if len(self.got) >= self.depth else a

    def send(self, a, dx, dy, dz):
        self.got.append(shift(self.turn(a), dx, dy, dz))
        return self.got[-1]

    def swap(self, a, pairs):
        self.got.append(lax.ppermute(self.turn(a), "island", pairs))
        return self.got[-1]


def local(
    tokens,
    cotangent,
    weight,
    moment_one,
    moment_two,
    step_count,
    outer_grad,
    outer_params,
    outer_moment,
):
    tok, cot, wgt = tokens[0], cotangent[0], weight[0]
    f32, bf16 = jnp.float32, jnp.bfloat16
    me = lax.axis_index("fsdp")
    pos = jnp.stack([me // (NY * NZ), (me // NZ) % NY, me % NZ]).astype(jnp.int32)

    wa, wb = wgt[:LANE], wgt[LANE:]

    all_a = lax.all_gather(wa, "fsdp", axis=0, tiled=True, axis_index_groups=GROUP_A)
    nb1 = shift(wb, -1, 0, 0)
    nb3 = shift(wb, 1, 0, 0)
    nb2 = shift(wb, 2, 0, 0)

    near_b = sums([(LANE, [(w, 0)]) for w in (wb, nb1, nb2, nb3)])
    tokv, inv, cots = stats(tok, cot)
    cots = after(cots, near_b)
    ga20, ga21, gb20, gb21 = grad_terms(
        pos, tokv, cots, [(0, 2, 0), (0, 2, 1), (1, 2, 0), (1, 2, 1)], "grad_far"
    )

    def add(*xs):
        return sums([(xs[0].shape[0], [(x, 0) for x in xs])])

    q = Queue(5)
    ra_p = q.send(ga20, 1, 0, 0)
    ra_m = q.send(ga21, -1, 0, 0)
    rb_p = q.send(gb20, 0, 0, 1)
    rb_m = q.send(gb21, 0, 0, -1)
    yb = q.send(near_b, 0, 1, 0)
    ga11, ga30, gb11, gb30, ga10, ga31, gb10, gb31 = grad_terms(
        pos,
        tokv,
        cots,
        [(0, 1, 1), (0, 3, 0), (1, 1, 1), (1, 3, 0), (0, 1, 0), (0, 3, 1), (1, 1, 0), (1, 3, 1)],
        "grad_next",
    )
    pa1 = q.send(ga11, 1, 0, 0)
    ma0 = q.send(ga30, -1, 0, 0)
    pb1 = q.send(gb11, 0, 0, 1)
    mb0 = q.send(gb30, 0, 0, -1)
    mine = outer_grad[0].astype(bf16)
    swapped = q.swap(mine, [(0, 1), (1, 0), (2, 3), (3, 2)])
    pa0 = q.send(add(ga10, ra_p), 1, 0, 0)
    ma1 = q.send(add(ga31, ra_m), -1, 0, 0)
    pb0 = q.send(add(gb10, rb_p), 0, 0, 1)
    mb1 = q.send(add(gb31, rb_m), 0, 0, -1)
    pair = add(mine, swapped)
    other = q.swap(pair, [(0, 2), (2, 0), (1, 3), (3, 1)])
    ga00, ga01, gb00, gb01 = grad_terms(
        pos, tokv, cots, [(0, 0, 0), (0, 0, 1), (1, 0, 0), (1, 0, 1)], "grad_own"
    )
    a0, a1 = all_a[:HALF], all_a[HALF:]
    wa31 = q.send(a1, 1, 0, 0)
    wa10 = q.send(a0, -1, 0, 0)
    wb31 = q.send(yb, 0, 0, 1)
    wb10 = q.send(near_b, 0, 0, -1)
    own = [(0, 0, 0), (0, 0, 1), (1, 0, 0), (1, 0, 1)]
    gh1, acc1 = gradh(pos, cot, tokv, own, [all_a, near_b, yb], "gradh_own")
    sb = q.send(after(add(gb01, pb1, mb1), acc1), 0, 1, 0)
    wa30 = q.send(a0, 1, 0, 0)
    wa11 = q.send(a1, -1, 0, 0)
    wb30 = q.send(near_b, 0, 0, 1)
    wb11 = q.send(yb, 0, 0, -1)
    wa21 = q.send(wa31, 1, 0, 0)
    wa20 = q.send(wa10, -1, 0, 0)
    wb21 = q.send(wb31, 0, 0, 1)
    wb20 = q.send(wb10, 0, 0, -1)

    grad_a = lax.psum_scatter(
        sums([(HALF, [(a, 0) for a in (ga00, pa0, ma0)]), (HALF, [(a, 0) for a in (ga01, pa1, ma1)])]),
        "fsdp",
        scatter_dimension=0,
        tiled=True,
        axis_index_groups=GROUP_A,
    )
    t0, t1, t2, t3 = sums(*[[(LANE, [(a, k * LANE) for a in (gb00, pb0, mb0, sb)])] for k in range(4)])
    d1 = q.send(t1, 1, 0, 0)
    d3 = q.send(t3, -1, 0, 0)
    d2 = q.send(t2, 2, 0, 0)
    grad_b = (t0.astype(f32) + d1.astype(f32)) + (d2.astype(f32) + d3.astype(f32))
    grad = jnp.concatenate([grad_a.astype(f32), grad_b], axis=0)

    one = [(0, 3, 1), (0, 1, 0), (1, 3, 1), (1, 1, 0)]
    two = [(0, 3, 0), (0, 1, 1), (1, 3, 0), (1, 1, 1)]
    far = [(0, 2, 1), (0, 2, 0), (1, 2, 1), (1, 2, 0)]
    gh2, acc2 = gradh(pos, cot, tokv, one, [wa31, wa10, wb31, wb10], "gradh_one")
    gh3, acc3 = gradh(pos, cot, tokv, two, [wa30, wa11, wb30, wb11], "gradh_two")
    input_grad = input_gradient(
        pos,
        inv,
        cot,
        tokv,
        (acc1, acc2, acc3),
        (gh1, gh2, gh3),
        (own, one, two),
        far,
        (wa21, wa20, wb21, wb20),
    )

    t_float = step_count[0].astype(f32)
    new_one = 0.9 * moment_one[0] + 0.1 * grad
    new_two = 0.95 * moment_two[0] + 0.05 * grad * grad
    corr_one = 1.0 - jnp.power(jnp.float32(0.9), t_float)
    corr_two = 1.0 - jnp.power(jnp.float32(0.95), t_float)
    update = new_one / corr_one / (jnp.sqrt(new_two / corr_two) + 1e-08)
    wf = wgt.astype(f32)
    new_w = (wf - 0.15 * (update + 0.1 * wf)).astype(bf16)

    delta = (pair.astype(f32) + other.astype(f32)) / lax.axis_size("island")
    new_moment = 0.9 * outer_moment + delta
    new_params = outer_params - 0.7 * (delta + 0.9 * new_moment)
    return (new_w[None], new_one[None], new_two[None], input_grad[None], new_params, new_moment)


def solution(mesh):
    rows, mine = P("island", "fsdp", None), P("fsdp", None)
    return jax.shard_map(
        local,
        mesh=mesh,
        in_specs=(rows, rows, rows, rows, rows, P("island"), rows, mine, mine),
        out_specs=(rows, rows, rows, rows, mine, mine),
        check_vma=False,
    )
```

time: 375 us -> 157 us (0.42)
  waiting for transfers between devices: 320 us -> 33.4 us
  starting transfers between devices: 0.12 us -> 51.5 us
  Pallas kernels: 0 us -> 35.1 us
  other arithmetic: 20.8 us -> 3.61 us
  matrix products: 16.7 us -> 0 us
  local copies, waits for them, and re-layouts: 0.53 us -> 16.4 us
    reduce_scatter x1, waiting for transfers between devices: 163 us -> 0.02 us  [local(): lax.psum_scatter(sums([(HALF, [(a, 0) for a in (ga00, pa0, ma0)]), (HALF,...]
    all_gather x1, waiting for transfers between devices: 108 us -> 0.02 us  [local(): lax.all_gather(wa, 'fsdp', axis=0, tiled=True, axis_index_groups=GROUP_A)]
    ppermute x0 -> x34, starting transfers between devices: none -> 51.4 us  [the longest x32 48.4 us: shift(): return lax.ppermute(a, 'fsdp', pairs)]
    psum x1 -> x0, waiting for transfers between devices: 48.6 us -> none  [outer_update(): lax.psum(outer_grad[0].astype(jnp.bfloat16), 'island').astype(jnp.float32)]
    pallas_call x0 -> x17, Pallas kernels: none -> 35.1 us  [the longest x3 10.6 us: gradh(): pl.pallas_call(functools.partial(gradh_kernel, parts, len(pieces)), in_sp...]
    ppermute x0 -> x34, waiting for transfers between devices: none -> 33.3 us  [the longest x32 33.3 us: shift(): return lax.ppermute(a, 'fsdp', pairs)]
    dot_general x2 -> x0, matrix products: 16.7 us -> none  [the longest x1 9.74 us: local(): jnp.einsum('tk,dk->td', cot, lax.all_gather(wgt, 'fsdp', axis=0, tiled=Tr...]
    unnamed x14 -> x60, local copies, waits for them, and re-layouts: 0.53 us -> 13.4 us
  transfers between devices with their start and end apart: 3 -> 36, of which waited for: 3 -> 7; matrix products, arithmetic and copies ran while one was open for 9% -> 2% of each run, Pallas kernels for 0% -> 23%
where the time goes in v1:
time: 157 us; the launch traced here: 155 us
  starting transfers between devices  51.5 us (33%)
  Pallas kernels  35.1 us (22%)
  waiting for transfers between devices  33.4 us (21%)
  local copies, waits for them, and re-layouts  16.4 us (10%)
  between operations  15.3 us (10%)
  other arithmetic  3.61 us (2%)
    ppermute x32, starting transfers between devices, shift(): return lax.ppermute(a, 'fsdp', pairs)  48.4 us
    ppermute x32, waiting for transfers between devices, shift(): return lax.ppermute(a, 'fsdp', pairs)  33.3 us
    unnamed x60, local copies, waits for them, and re-layouts  13.4 us
    pallas_call x3, Pallas kernels, gradh(): pl.pallas_call(functools.partial(gradh_kernel, parts, len(pieces)), in_sp...  10.6 us
    pallas_call x1, Pallas kernels, input_gradient(): pl.pallas_call(functools.partial(input_kernel, parts, last, len(accs)), i...  10.3 us
    pallas_call x3, Pallas kernels, grad_terms(): pl.pallas_call(functools.partial(grad_kernel, parts), in_specs=[SMEM, VME...  6.65 us
    pallas_call x9, Pallas kernels, sums(): pl.pallas_call(functools.partial(sum_kernel, plan, len(arrays)), in_specs...  4.39 us
    pallas_call x1, Pallas kernels, stats(): pl.pallas_call(stats_kernel, in_specs=[pl.BlockSpec(memory_space=pltpu.HB...  3.16 us
  transfers between devices with their start and end apart: 36, of which 7 were waited for; matrix products, arithmetic and copies ran while one was open for 2% of the time, Pallas kernels for 23%

profile of v1, /device:TPU:0, one launch (start us, length us, event | category | flops | bytes accessed | tf_op | source)
XLA Modules:
  0.0 155.2 jit_solution(8760556315005171150)
XLA Ops:
  7.2 1.6 %fusion.5 = (bf16[1,128,512]{2,1,0:T(8,128)(2,1)}, bf16[128,512]{1,0:T(8,128)(2,1)S(1)}) fusion(bf16[1,256,512]{2,1,0:T(8,128)(2,1)} %param.11), kind=kLoop, calls=%fused_computation.19 | loop fusion | bytes 524288 | tf_op jit(solution)/shard_map/slice | solution.py:343
  8.9 2.9 %collective-permute-start = (bf16[128,512]{1,0:T(8,128)(2,1)S(1)}, bf16[128,512]{1,0:T(8,128)(2,1)S(1)}, u32[]{:S(2)}, u32[]{:S(2)}) collective-permute-start(bf16[128,512]{1,0:T(8,128)(2,1)S(1)} %get-tuple-element.128.refs_0_), channel_id=1, source_target_pairs={{0,24},{1,25},{2,26},{3,27},{4,28},{5,29},{6,30},{7,31},{8,0},{9,1... | collective-permute-start | bytes 393224 | tf_op jit(solution)/shard_map/ppermute | solution.py:40
  14.6 3.4 %copy-done.4 = bf16[1,512,8192]{2,1,0:T(8,128)(2,1)S(1)} copy-done((bf16[1,512,8192]{2,1,0:T(8,128)(2,1)S(1)}, bf16[1,512,8192]{2,1,0:T(8,128)(2,1)}, u32[]{:S(2)}) %copy-start.4) | copy-done | bytes 8388632
  17.9 3.2 %token_stats.1 = (bf16[512,8192]{1,0:T(8,128)(2,1)S(1)}, f32[512,128]{1,0:T(8,128)S(1)}, bf16[512,512]{1,0:T(8,128)(2,1)S(1)}) custom-call(bf16[512,8192]{1,0:T(8,128)(2,1)S(1)} %bitcast.27, bf16[512,512]{1,0:T(8,128)(2,1)S(1)} %bitcast.22), custom_call_target="tpu_custom_call" | custom-call | flops 12582912 | bytes 10485760 | tf_op jit(solution)/shard_map/token_stats/pallas_call | solution.py:87
  22.0 1.8 %grad_far.1 = (bf16[512,512]{1,0:T(8,128)(2,1)S(1)}, bf16[512,512]{1,0:T(8,128)(2,1)S(1)}, bf16[512,512]{1,0:T(8,128)(2,1)S(1)}, bf16[512,512]{1,0:T(8,128)(2,1)S(1)}) custom-call(s32[3]{0:T(128)S(1)} %pad_add_fusion.pos_ref, bf16[512,8192]{1,0:T(8,128)(2,1)S(1)} %get-tuple-element.63.tokv_ref, bf16[512,512]{1,0:T(8,128)(2,1)S(1)} %get-tuple-element.65.cots_ref), custom_call_target="tpu_custom_call" | custom-call | flops 1073741824 | bytes 4194304 | tf_op jit(solution)/shard_map/grad_far/pallas_call | solution.py:116
  23.8 2.0 %collective-permute-start.9 = (bf16[512,512]{1,0:T(8,128)(2,1)S(1)}, bf16[512,512]{1,0:T(8,128)(2,1)S(1)}, u32[]{:S(2)}, u32[]{:S(2)}) collective-permute-start(bf16[512,512]{1,0:T(8,128)(2,1)S(1)} %get-tuple-element.80), channel_id=1, source_target_pairs={{0,1},{1,2},{2,3},{3,0},{4,5},{5,6},{6,7},{7,4},{8,9},{9,10},{10,1... | collective-permute-start | bytes 1572872 | tf_op jit(solution)/shard_map/ppermute | solution.py:40
  25.8 1.8 %collective-permute-start.3 = (bf16[512,512]{1,0:T(8,128)(2,1)S(1)}, bf16[512,512]{1,0:T(8,128)(2,1)S(1)}, u32[]{:S(2)}, u32[]{:S(2)}) collective-permute-start(bf16[512,512]{1,0:T(8,128)(2,1)S(1)} %get-tuple-element.68), channel_id=1, source_target_pairs={{0,8},{1,9},{2,10},{3,11},{4,12},{5,13},{6,14},{7,15},{8,16},{9,17... | collective-permute-start | bytes 1572872 | tf_op jit(solution)/shard_map/ppermute | solution.py:40
  29.1 2.2 %collective-permute-start.12 = (bf16[512,512]{1,0:T(8,128)(2,1)S(1)}, bf16[512,512]{1,0:T(8,128)(2,1)S(1)}, u32[]{:S(2)}, u32[]{:S(2)}) collective-permute-start(bf16[512,512]{1,0:T(8,128)(2,1)S(1)} %get-tuple-element.85), channel_id=1, source_target_pairs={{0,3},{1,0},{2,1},{3,2},{4,7},{5,4},{6,5},{7,6},{8,11},{9,8},{10,9... | collective-permute-start | bytes 1572872 | tf_op jit(solution)/shard_map/ppermute | solution.py:40
  31.3 3.0 %grad_next.1 = (bf16[512,512]{1,0:T(8,128)(2,1)S(1)}, bf16[512,512]{1,0:T(8,128)(2,1)S(1)}, bf16[512,512]{1,0:T(8,128)(2,1)S(1)}, bf16[512,512]{1,0:T(8,128)(2,1...) custom-call(s32[3]{0:T(128)S(1)} %pad_add_fusion.pos_ref, ...), custom_call_target="tpu_custom_call" | custom-call | flops 2147483648 | bytes 8388608 | tf_op jit(solution)/shard_map/grad_next/pallas_call | solution.py:116
  34.2 12.5 %collective-permute-done.9.refs_1_ = bf16[512,512]{1,0:T(8,128)(2,1)S(1)} collective-permute-done((bf16[512,512]{1,0:T(8,128)(2,1)S(1)}, bf16[512,512]{1,0:T(8,128)(2,1)S(1)}, u32[]{:S(2)}, u32[]{:S(2)}) %collective-permute-start.9) | collective-permute-done | bytes 524320 | tf_op jit(solution)/shard_map/ppermute | solution.py:40
  46.8 1.7 %collective-permute-start.4 = (bf16[512,512]{1,0:T(8,128)(2,1)S(1)}, bf16[512,512]{1,0:T(8,128)(2,1)S(1)}, u32[]{:S(2)}, u32[]{:S(2)}) collective-permute-start(bf16[512,512]{1,0:T(8,128)(2,1)S(1)} %get-tuple-element.70), channel_id=1, source_target_pairs={{0,8},{1,9},{2,10},{3,11},{4,12},{5,13},{6,14},{7,15},{8,16},{9,17... | collective-permute-start | bytes 1572872 | tf_op jit(solution)/shard_map/ppermute | solution.py:40
  48.4 1.6 %collective-permute-start.7 = (bf16[512,512]{1,0:T(8,128)(2,1)S(1)}, bf16[512,512]{1,0:T(8,128)(2,1)S(1)}, u32[]{:S(2)}, u32[]{:S(2)}) collective-permute-start(bf16[512,512]{1,0:T(8,128)(2,1)S(1)} %get-tuple-element.74), channel_id=1, source_target_pairs={{0,24},{1,25},{2,26},{3,27},{4,28},{5,29},{6,30},{7,31},{8,0},{9,1... | collective-permute-start | bytes 1572872 | tf_op jit(solution)/shard_map/ppermute | solution.py:40
  51.2 3.2 %collective-permute-start.13 = (bf16[512,512]{1,0:T(8,128)(2,1)S(1)}, bf16[512,512]{1,0:T(8,128)(2,1)S(1)}, u32[]{:S(2)}, u32[]{:S(2)}) collective-permute-start(bf16[512,512]{1,0:T(8,128)(2,1)S(1)} %get-tuple-element.86), channel_id=1, source_target_pairs={{0,3},{1,0},{2,1},{3,2},{4,7},{5,4},{6,5},{7,6},{8,11},{9,8},{10,9... | collective-permute-start | bytes 1572872 | tf_op jit(solution)/shard_map/ppermute | solution.py:40
  54.8 6.5 %collective-permute-done.10.refs_1_ = bf16[512,512]{1,0:T(8,128)(2,1)S(1)} collective-permute-done((bf16[512,512]{1,0:T(8,128)(2,1)S(1)}, bf16[512,512]{1,0:T(8,128)(2,1)S(1)}, u32[]{:S(2)}, u32[]{:S(2)}) %collective-permute-start.10) | collective-permute-done | bytes 524320 | tf_op jit(solution)/shard_map/ppermute | solution.py:40
  63.5 1.8 %collective-permute-start.8 = (bf16[512,512]{1,0:T(8,128)(2,1)S(1)}, bf16[512,512]{1,0:T(8,128)(2,1)S(1)}, u32[]{:S(2)}, u32[]{:S(2)}) collective-permute-start(bf16[512,512]{1,0:T(8,128)(2,1)S(1)} %sum_terms.11), channel_id=1, source_target_pairs={{0,24},{1,25},{2,26},{3,27},{4,28},{5,29},{6,30},{7,31},{8,0},{9,1... | collective-permute-start | bytes 1572872 | tf_op jit(solution)/shard_map/ppermute | solution.py:40
  65.4 1.8 %grad_own.1 = (bf16[512,512]{1,0:T(8,128)(2,1)S(1)}, bf16[512,512]{1,0:T(8,128)(2,1)S(1)}, bf16[512,512]{1,0:T(8,128)(2,1)S(1)}, bf16[512,512]{1,0:T(8,128)(2,1)S(1)}) custom-call(s32[3]{0:T(128)S(1)} %pad_add_fusion.pos_ref, bf16[512,8192]{1,0:T(8,128)(2,1)S(1)} %get-tuple-element.63.tokv_ref, bf16[512,512]{1,0:T(8,128)(2,1)S(1)} %get-tuple-element.65.cots_ref), custom_call_target="tpu_custom_call" | custom-call | flops 1073741824 | bytes 4194304 | tf_op jit(solution)/shard_map/grad_own/pallas_call | solution.py:116
  68.2 3.3 %collective-permute-start.14 = (bf16[512,512]{1,0:T(8,128)(2,1)S(1)}, bf16[512,512]{1,0:T(8,128)(2,1)}, u32[]{:S(2)}, u32[]{:S(2)}) collective-permute-start(bf16[512,512]{1,0:T(8,128)(2,1)S(1)} %sum_terms.14), channel_id=1, source_target_pairs={{0,3},{1,0},{2,1},{3,2},{4,7},{5,4},{6,5},{7,6},{8,11},{9,8},{10,9... | collective-permute-start | bytes 1572872 | tf_op jit(solution)/shard_map/ppermute | solution.py:40
  71.5 4.2 %collective-permute-done.11.refs_1_ = bf16[512,512]{1,0:T(8,128)(2,1)S(1)} collective-permute-done((bf16[512,512]{1,0:T(8,128)(2,1)S(1)}, bf16[512,512]{1,0:T(8,128)(2,1)S(1)}, u32[]{:S(2)}, u32[]{:S(2)}) %collective-permute-start.11) | collective-permute-done | bytes 524320 | tf_op jit(solution)/shard_map/ppermute | solution.py:40
  79.8 2.0 %collective-permute-start.22 = (bf16[512,512]{1,0:T(8,128)(2,1)S(1)}, bf16[512,512]{1,0:T(8,128)(2,1)S(1)}, u32[]{:S(2)}, u32[]{:S(2)}) collective-permute-start(bf16[512,512]{1,0:T(8,128)(2,1)S(1)} %get-tuple-element.103), channel_id=1, source_target_pairs={{0,24},{1,25},{2,26},{3,27},{4,28},{5,29},{6,30},{7,31},{8,0},{9,1... | collective-permute-start | bytes 1572872 | tf_op jit(solution)/shard_map/ppermute | solution.py:40
  82.8 3.0 %collective-permute-start.17 = (bf16[256,512]{1,0:T(8,128)(2,1)S(1)}, bf16[256,512]{1,0:T(8,128)(2,1)S(1)}, u32[]{:S(2)}, u32[]{:S(2)}) collective-permute-start(bf16[256,512]{1,0:T(8,128)(2,1)S(1)} %sum_terms.16), channel_id=1, source_target_pairs={{0,64},{64,0},{32,96},{96,32},{1,65},{65,1},{33,97},{97,33},{2,66}... | collective-permute-start | bytes 786440 | tf_op jit(solution)/shard_map/ppermute | solution.py:323
  85.8 3.1 %collective-permute-start.19 = (bf16[512,512]{1,0:T(8,128)(2,1)S(1)}, bf16[512,512]{1,0:T(8,128)(2,1)S(1)}, u32[]{:S(2)}, u32[]{:S(2)}) collective-permute-start(bf16[512,512]{1,0:T(8,128)(2,1)S(1)} %sum_terms.9.rest_1_), channel_id=1, source_target_pairs={{0,3},{1,0},{2,1},{3,2},{4,7},{5,4},{6,5},{7,6},{8,11},{9,8},{10,9... | collective-permute-start | bytes 1572872 | tf_op jit(solution)/shard_map/ppermute | solution.py:40
  92.3 3.4 %copy-done.1 = bf16[512,8192]{1,0:T(8,128)(2,1)S(1)} copy-done((bf16[512,8192]{1,0:T(8,128)(2,1)S(1)}, bf16[512,8192]{1,0:T(8,128)(2,1)}, u32[]{:S(2)}) %copy-start.1) | copy-done | bytes 8388632
  95.7 3.5 %gradh_own.1 = (bf16[512,2048]{1,0:T(8,128)(2,1)S(1)}, f32[512,128]{1,0:T(8,128)S(1)}) custom-call(s32[3]{0:T(128)S(1)} %pad_add_fusion.pos_ref, bf16[512,512]{1,0:T(8,128)(2,1)S(1)} %bitcast.23, bf16[512,8192]{1,0:T(8,128)(2,1)S(1)} %copy-done.1, bf16[1024,512]{1,0:T(8,128)(2,1)} %bitcast.29, bf16[512,512]{1,0:T(8,128)(2,1)} %copy-done.5, ...), custom_call_target="tpu_custom_call" | custom-call | flops 1073741824 | bytes 4194304 | tf_op jit(solution)/shard_map/gradh_own/pallas_call | solution.py:166
  100.0 2.9 %collective-permute-start.30 = (bf16[512,512]{1,0:T(8,128)(2,1)S(1)}, bf16[512,512]{1,0:T(8,128)(2,1)S(1)}, u32[]{:S(2)}, u32[]{:S(2)}) collective-permute-start(bf16[512,512]{1,0:T(8,128)(2,1)S(1)} %get-tuple-element.112), channel_id=1, source_target_pairs={{0,24},{1,25},{2,26},{3,27},{4,28},{5,29},{6,30},{7,31},{8,0},{9,1... | collective-permute-start | bytes 1572872 | tf_op jit(solution)/shard_map/ppermute | solution.py:40
  104.4 3.9 %collective-permute-start.20 = (bf16[512,512]{1,0:T(8,128)(2,1)}, bf16[512,512]{1,0:T(8,128)(2,1)S(1)}, u32[]{:S(2)}, u32[]{:S(2)}) collective-permute-start(bf16[512,512]{1,0:T(8,128)(2,1)} %collective-permute-done.15.rest_2_), channel_id=1, source_target_pairs={{0,3},{1,0},{2,1},{3,2},{4,7},{5,4},{6,5},{7,6},{8,11},{9,8},{10,9... | collective-permute-start | bytes 1572872 | tf_op jit(solution)/shard_map/ppermute | solution.py:40
  108.3 7.4 %collective-permute-done.18.refs_3_ = bf16[512,512]{1,0:T(8,128)(2,1)S(1)} collective-permute-done((bf16[512,512]{1,0:T(8,128)(2,1)S(1)}, bf16[512,512]{1,0:T(8,128)(2,1)S(1)}, u32[]{:S(2)}, u32[]{:S(2)}) %collective-permute-start.18) | collective-permute-done | bytes 524320 | tf_op jit(solution)/shard_map/ppermute | solution.py:40
  117.2 2.6 %collective-permute-start.25 = (bf16[512,512]{1,0:T(8,128)(2,1)S(1)}, bf16[512,512]{1,0:T(8,128)(2,1)S(1)}, u32[]{:S(2)}, u32[]{:S(2)}) collective-permute-start(bf16[512,512]{1,0:T(8,128)(2,1)S(1)} %collective-permute-done.22.rest_1_), channel_id=1, source_target_pairs={{0,24},{1,25},{2,26},{3,27},{4,28},{5,29},{6,30},{7,31},{8,0},{9,1... | collective-permute-start | bytes 1572872 | tf_op jit(solution)/shard_map/ppermute | solution.py:40
  120.1 1.6 %collective-permute-start.32 = (bf16[512,512]{1,0:T(8,128)(2,1)}, bf16[512,512]{1,0:T(8,128)(2,1)S(1)}, u32[]{:S(2)}, u32[]{:S(2)}) collective-permute-start(bf16[512,512]{1,0:T(8,128)(2,1)} %collective-permute-done.29.rest_2_), channel_id=1, source_target_pairs={{0,1},{1,2},{2,3},{3,0},{4,5},{5,6},{6,7},{7,4},{8,9},{9,10},{10,1... | collective-permute-start | bytes 1572872 | tf_op jit(solution)/shard_map/ppermute | solution.py:40
  124.0 3.5 %gradh_one.1 = (bf16[512,2048]{1,0:T(8,128)(2,1)S(1)}, f32[512,128]{1,0:T(8,128)S(1)}) custom-call(s32[3]{0:T(128)S(1)} %pad_add_fusion.pos_ref, bf16[512,512]{1,0:T(8,128)(2,1)S(1)} %bitcast.24, bf16[512,8192]{1,0:T(8,128)(2,1)S(1)} %copy-done.1, bf16[512,512]{1,0:T(8,128)(2,1)} %copy-done.17, bf16[512,512]{1,0:T(8,128)(2,1)} %copy-done.16, ...), custom_call_target="tpu_custom_call" | custom-call | flops 1073741824 | bytes 4194304 | tf_op jit(solution)/shard_map/gradh_one/pallas_call | solution.py:166
  127.8 3.1 %collective-permute-start.28 = (bf16[128,512]{1,0:T(8,128)(2,1)S(1)}, bf16[128,512]{1,0:T(8,128)(2,1)S(1)}, u32[]{:S(2)}, u32[]{:S(2)}) collective-permute-start(bf16[128,512]{1,0:T(8,128)(2,1)S(1)} %get-tuple-element.108), channel_id=1, source_target_pairs={{0,24},{1,25},{2,26},{3,27},{4,28},{5,29},{6,30},{7,31},{8,0},{9,1... | collective-permute-start | bytes 393224 | tf_op jit(solution)/shard_map/ppermute | solution.py:40
  130.9 3.5 %gradh_two.1 = (bf16[512,2048]{1,0:T(8,128)(2,1)S(1)}, f32[512,128]{1,0:T(8,128)S(1)}) custom-call(s32[3]{0:T(128)S(1)} %pad_add_fusion.pos_ref, bf16[512,512]{1,0:T(8,128)(2,1)S(1)} %bitcast.25, bf16[512,8192]{1,0:T(8,128)(2,1)S(1)} %copy-done.1, bf16[512,512]{1,0:T(8,128)(2,1)} %copy-done.21, bf16[512,512]{1,0:T(8,128)(2,1)} %copy-done.23, ...), custom_call_target="tpu_custom_call" | custom-call | flops 1073741824 | bytes 4194304 | tf_op jit(solution)/shard_map/gradh_two/pallas_call | solution.py:166
  135.6 10.3 %input_gradient.1 = bf16[512,8192]{1,0:T(8,128)(2,1)} custom-call(s32[3]{0:T(128)S(1)} %pad_add_fusion.pos_ref, f32[512,128]{1,0:T(8,128)S(1)} %copy-done.12, bf16[512,512]{1,0:T(8,128)(2,1)S(1)} %bitcast.26, bf16[512,8192]{1,0:T(8,128)(2,1)S(1)} %copy-done.1, f32[512,128]{1,0:T(8,128)S(1)} %get-tuple-element.90.rest_0_, ...), custom_call_target="tpu_custom_call" | custom-call | flops 2147483648 | bytes 25165824 | tf_op jit(solution)/shard_map/input_gradient/pallas_call | solution.py:246
  (127 shorter events, 27.5 us)
Async XLA Ops:
  7.2 69.9 %all-gather.3.cloned.1.call-start = ((), (), s32[]{:S(2)}) async-start(), calls=%async_computation.2 | async-start | bytes 1179648 | tf_op jit(solution)/shard_map/all_gather | solution.py:345
  8.9 137.2 %reduce-scatter.2.cloned.1.call-start = ((), (), s32[]{:S(2)}) async-start(), calls=%async_computation.1 | async-start | bytes 1179648 | tf_op jit(solution)/shard_map/reduce_scatter | solution.py:405
  8.9 13.0 %collective-permute-start = (bf16[128,512]{1,0:T(8,128)(2,1)S(1)}, bf16[128,512]{1,0:T(8,128)(2,1)S(1)}, u32[]{:S(2)}, u32[]{:S(2)}) collective-permute-start(bf16[128,512]{1,0:T(8,128)(2,1)S(1)} %get-tuple-element.128.refs_0_), channel_id=1, source_target_pairs={{0,24},{1,25},{2,26},{3,27},{4,28},{5,29},{6,30},{7,31},{8,0},{9,1... | collective-permute-start | bytes 393224 | tf_op jit(solution)/shard_map/ppermute | solution.py:40
  23.8 22.9 %collective-permute-start.9 = (bf16[512,512]{1,0:T(8,128)(2,1)S(1)}, bf16[512,512]{1,0:T(8,128)(2,1)S(1)}, u32[]{:S(2)}, u32[]{:S(2)}) collective-permute-start(bf16[512,512]{1,0:T(8,128)(2,1)S(1)} %get-tuple-element.80), channel_id=1, source_target_pairs={{0,1},{1,2},{2,3},{3,0},{4,5},{5,6},{6,7},{7,4},{8,9},{9,10},{10,1... | collective-permute-start | bytes 1572872 | tf_op jit(solution)/shard_map/ppermute | solution.py:40
  25.8 20.9 %collective-permute-start.3 = (bf16[512,512]{1,0:T(8,128)(2,1)S(1)}, bf16[512,512]{1,0:T(8,128)(2,1)S(1)}, u32[]{:S(2)}, u32[]{:S(2)}) collective-permute-start(bf16[512,512]{1,0:T(8,128)(2,1)S(1)} %get-tuple-element.68), channel_id=1, source_target_pairs={{0,8},{1,9},{2,10},{3,11},{4,12},{5,13},{6,14},{7,15},{8,16},{9,17... | collective-permute-start | bytes 1572872 | tf_op jit(solution)/shard_map/ppermute | solution.py:40
  27.6 20.8 %collective-permute-start.6 = (bf16[512,512]{1,0:T(8,128)(2,1)S(1)}, bf16[512,512]{1,0:T(8,128)(2,1)S(1)}, u32[]{:S(2)}, u32[]{:S(2)}) collective-permute-start(bf16[512,512]{1,0:T(8,128)(2,1)S(1)} %get-tuple-element.73), channel_id=1, source_target_pairs={{0,24},{1,25},{2,26},{3,27},{4,28},{5,29},{6,30},{7,31},{8,0},{9,1... | collective-permute-start | bytes 1572872 | tf_op jit(solution)/shard_map/ppermute | solution.py:40
  29.1 22.1 %collective-permute-start.12 = (bf16[512,512]{1,0:T(8,128)(2,1)S(1)}, bf16[512,512]{1,0:T(8,128)(2,1)S(1)}, u32[]{:S(2)}, u32[]{:S(2)}) collective-permute-start(bf16[512,512]{1,0:T(8,128)(2,1)S(1)} %get-tuple-element.85), channel_id=1, source_target_pairs={{0,3},{1,0},{2,1},{3,2},{4,7},{5,4},{6,5},{7,6},{8,11},{9,8},{10,9... | collective-permute-start | bytes 1572872 | tf_op jit(solution)/shard_map/ppermute | solution.py:40
  46.7 14.5 %collective-permute-start.10 = (bf16[512,512]{1,0:T(8,128)(2,1)S(1)}, bf16[512,512]{1,0:T(8,128)(2,1)S(1)}, u32[]{:S(2)}, u32[]{:S(2)}) collective-permute-start(bf16[512,512]{1,0:T(8,128)(2,1)S(1)} %get-tuple-element.82), channel_id=1, source_target_pairs={{0,1},{1,2},{2,3},{3,0},{4,5},{5,6},{6,7},{7,4},{8,9},{9,10},{10,1... | collective-permute-start | bytes 1572872 | tf_op jit(solution)/shard_map/ppermute | solution.py:40
  46.8 15.3 %collective-permute-start.4 = (bf16[512,512]{1,0:T(8,128)(2,1)S(1)}, bf16[512,512]{1,0:T(8,128)(2,1)S(1)}, u32[]{:S(2)}, u32[]{:S(2)}) collective-permute-start(bf16[512,512]{1,0:T(8,128)(2,1)S(1)} %get-tuple-element.70), channel_id=1, source_target_pairs={{0,8},{1,9},{2,10},{3,11},{4,12},{5,13},{6,14},{7,15},{8,16},{9,17... | collective-permute-start | bytes 1572872 | tf_op jit(solution)/shard_map/ppermute | solution.py:40
  48.4 15.1 %collective-permute-start.7 = (bf16[512,512]{1,0:T(8,128)(2,1)S(1)}, bf16[512,512]{1,0:T(8,128)(2,1)S(1)}, u32[]{:S(2)}, u32[]{:S(2)}) collective-permute-start(bf16[512,512]{1,0:T(8,128)(2,1)S(1)} %get-tuple-element.74), channel_id=1, source_target_pairs={{0,24},{1,25},{2,26},{3,27},{4,28},{5,29},{6,30},{7,31},{8,0},{9,1... | collective-permute-start | bytes 1572872 | tf_op jit(solution)/shard_map/ppermute | solution.py:40
  50.0 18.0 %collective-permute-start.15 = (bf16[512,512]{1,0:T(8,128)(2,1)S(1)}, bf16[512,512]{1,0:T(8,128)(2,1)}, u32[]{:S(2)}, u32[]{:S(2)}) collective-permute-start(bf16[512,512]{1,0:T(8,128)(2,1)S(1)} %sum_terms.9.rest_1_), channel_id=1, source_target_pairs={{0,4},{1,5},{2,6},{3,7},{4,0},{5,1},{6,2},{7,3},{8,12},{9,13},{10,... | collective-permute-start | bytes 1572872 | tf_op jit(solution)/shard_map/ppermute | solution.py:40
  51.2 17.0 %collective-permute-start.13 = (bf16[512,512]{1,0:T(8,128)(2,1)S(1)}, bf16[512,512]{1,0:T(8,128)(2,1)S(1)}, u32[]{:S(2)}, u32[]{:S(2)}) collective-permute-start(bf16[512,512]{1,0:T(8,128)(2,1)S(1)} %get-tuple-element.86), channel_id=1, source_target_pairs={{0,3},{1,0},{2,1},{3,2},{4,7},{5,4},{6,5},{7,6},{8,11},{9,8},{10,9... | collective-permute-start | bytes 1572872 | tf_op jit(solution)/shard_map/ppermute | solution.py:40
  62.1 13.6 %collective-permute-start.11 = (bf16[512,512]{1,0:T(8,128)(2,1)S(1)}, bf16[512,512]{1,0:T(8,128)(2,1)S(1)}, u32[]{:S(2)}, u32[]{:S(2)}) collective-permute-start(bf16[512,512]{1,0:T(8,128)(2,1)S(1)} %sum_terms.13), channel_id=1, source_target_pairs={{0,1},{1,2},{2,3},{3,0},{4,5},{5,6},{6,7},{7,4},{8,9},{9,10},{10,1... | collective-permute-start | bytes 1572872 | tf_op jit(solution)/shard_map/ppermute | solution.py:40
  62.1 13.6 %collective-permute-start.5 = (bf16[512,512]{1,0:T(8,128)(2,1)S(1)}, bf16[512,512]{1,0:T(8,128)(2,1)S(1)}, u32[]{:S(2)}, u32[]{:S(2)}) collective-permute-start(bf16[512,512]{1,0:T(8,128)(2,1)S(1)} %sum_terms.10), channel_id=1, source_target_pairs={{0,8},{1,9},{2,10},{3,11},{4,12},{5,13},{6,14},{7,15},{8,16},{9,17... | collective-permute-start | bytes 1572872 | tf_op jit(solution)/shard_map/ppermute | solution.py:40
  63.5 12.2 %collective-permute-start.8 = (bf16[512,512]{1,0:T(8,128)(2,1)S(1)}, bf16[512,512]{1,0:T(8,128)(2,1)S(1)}, u32[]{:S(2)}, u32[]{:S(2)}) collective-permute-start(bf16[512,512]{1,0:T(8,128)(2,1)S(1)} %sum_terms.11), channel_id=1, source_target_pairs={{0,24},{1,25},{2,26},{3,27},{4,28},{5,29},{6,30},{7,31},{8,0},{9,1... | collective-permute-start | bytes 1572872 | tf_op jit(solution)/shard_map/ppermute | solution.py:40
  68.0 13.8 %collective-permute-start.16 = (bf16[256,512]{1,0:T(8,128)(2,1)S(1)}, bf16[256,512]{1,0:T(8,128)(2,1)}, u32[]{:S(2)}, u32[]{:S(2)}) collective-permute-start(bf16[256,512]{1,0:T(8,128)(2,1)S(1)} %convert_bitcast_fusion.refs_0_), channel_id=1, source_target_pairs={{0,32},{32,0},{64,96},{96,64},{1,33},{33,1},{65,97},{97,65},{2,34}... | collective-permute-start | bytes 786440 | tf_op jit(solution)/shard_map/ppermute | solution.py:323
  68.2 17.7 %collective-permute-start.14 = (bf16[512,512]{1,0:T(8,128)(2,1)S(1)}, bf16[512,512]{1,0:T(8,128)(2,1)}, u32[]{:S(2)}, u32[]{:S(2)}) collective-permute-start(bf16[512,512]{1,0:T(8,128)(2,1)S(1)} %sum_terms.14), channel_id=1, source_target_pairs={{0,3},{1,0},{2,1},{3,2},{4,7},{5,4},{6,5},{7,6},{8,11},{9,8},{10,9... | collective-permute-start | bytes 1572872 | tf_op jit(solution)/shard_map/ppermute | solution.py:40
  75.7 23.9 %collective-permute-start.29 = (bf16[512,512]{1,0:T(8,128)(2,1)}, bf16[512,512]{1,0:T(8,128)(2,1)}, u32[]{:S(2)}, u32[]{:S(2)}) collective-permute-start(bf16[512,512]{1,0:T(8,128)(2,1)} %collective-permute-done.15.rest_2_), channel_id=1, source_target_pairs={{0,1},{1,2},{2,3},{3,0},{4,5},{5,6},{6,7},{7,4},{8,9},{9,10},{10,1... | collective-permute-start | bytes 1572872 | tf_op jit(solution)/shard_map/ppermute | solution.py:40
  78.5 21.1 %collective-permute-start.23 = (bf16[512,512]{1,0:T(8,128)(2,1)S(1)}, bf16[512,512]{1,0:T(8,128)(2,1)S(1)}, u32[]{:S(2)}, u32[]{:S(2)}) collective-permute-start(bf16[512,512]{1,0:T(8,128)(2,1)S(1)} %get-tuple-element.112), channel_id=1, source_target_pairs={{0,8},{1,9},{2,10},{3,11},{4,12},{5,13},{6,14},{7,15},{8,16},{9,17... | collective-permute-start | bytes 1572872 | tf_op jit(solution)/shard_map/ppermute | solution.py:40
  79.8 20.3 %collective-permute-start.22 = (bf16[512,512]{1,0:T(8,128)(2,1)S(1)}, bf16[512,512]{1,0:T(8,128)(2,1)S(1)}, u32[]{:S(2)}, u32[]{:S(2)}) collective-permute-start(bf16[512,512]{1,0:T(8,128)(2,1)S(1)} %get-tuple-element.103), channel_id=1, source_target_pairs={{0,24},{1,25},{2,26},{3,27},{4,28},{5,29},{6,30},{7,31},{8,0},{9,1... | collective-permute-start | bytes 1572872 | tf_op jit(solution)/shard_map/ppermute | solution.py:40
  82.8 16.4 %collective-permute-start.17 = (bf16[256,512]{1,0:T(8,128)(2,1)S(1)}, bf16[256,512]{1,0:T(8,128)(2,1)S(1)}, u32[]{:S(2)}, u32[]{:S(2)}) collective-permute-start(bf16[256,512]{1,0:T(8,128)(2,1)S(1)} %sum_terms.16), channel_id=1, source_target_pairs={{0,64},{64,0},{32,96},{96,32},{1,65},{65,1},{33,97},{97,33},{2,66}... | collective-permute-start | bytes 786440 | tf_op jit(solution)/shard_map/ppermute | solution.py:323
  85.8 18.6 %collective-permute-start.19 = (bf16[512,512]{1,0:T(8,128)(2,1)S(1)}, bf16[512,512]{1,0:T(8,128)(2,1)S(1)}, u32[]{:S(2)}, u32[]{:S(2)}) collective-permute-start(bf16[512,512]{1,0:T(8,128)(2,1)S(1)} %sum_terms.9.rest_1_), channel_id=1, source_target_pairs={{0,3},{1,0},{2,1},{3,2},{4,7},{5,4},{6,5},{7,6},{8,11},{9,8},{10,9... | collective-permute-start | bytes 1572872 | tf_op jit(solution)/shard_map/ppermute | solution.py:40
  99.3 16.5 %collective-permute-start.18 = (bf16[512,512]{1,0:T(8,128)(2,1)S(1)}, bf16[512,512]{1,0:T(8,128)(2,1)S(1)}, u32[]{:S(2)}, u32[]{:S(2)}) collective-permute-start(bf16[512,512]{1,0:T(8,128)(2,1)S(1)} %sum_terms.15), channel_id=1, source_target_pairs={{0,4},{1,5},{2,6},{3,7},{4,0},{5,1},{6,2},{7,3},{8,12},{9,13},{10,... | collective-permute-start | bytes 1572872 | tf_op jit(solution)/shard_map/ppermute | solution.py:40
  99.5 17.6 %collective-permute-start.31 = (bf16[512,512]{1,0:T(8,128)(2,1)S(1)}, bf16[512,512]{1,0:T(8,128)(2,1)S(1)}, u32[]{:S(2)}, u32[]{:S(2)}) collective-permute-start(bf16[512,512]{1,0:T(8,128)(2,1)S(1)} %copy-done.6), channel_id=1, source_target_pairs={{0,1},{1,2},{2,3},{3,0},{4,5},{5,6},{6,7},{7,4},{8,9},{9,10},{10,1... | collective-permute-start | bytes 1572872 | tf_op jit(solution)/shard_map/ppermute | solution.py:40
  99.6 17.6 %collective-permute-start.24 = (bf16[512,512]{1,0:T(8,128)(2,1)S(1)}, bf16[512,512]{1,0:T(8,128)(2,1)S(1)}, u32[]{:S(2)}, u32[]{:S(2)}) collective-permute-start(bf16[512,512]{1,0:T(8,128)(2,1)S(1)} %get-tuple-element.103), channel_id=1, source_target_pairs={{0,8},{1,9},{2,10},{3,11},{4,12},{5,13},{6,14},{7,15},{8,16},{9,17... | collective-permute-start | bytes 1572872 | tf_op jit(solution)/shard_map/ppermute | solution.py:40
  100.0 20.1 %collective-permute-start.30 = (bf16[512,512]{1,0:T(8,128)(2,1)S(1)}, bf16[512,512]{1,0:T(8,128)(2,1)S(1)}, u32[]{:S(2)}, u32[]{:S(2)}) collective-permute-start(bf16[512,512]{1,0:T(8,128)(2,1)S(1)} %get-tuple-element.112), channel_id=1, source_target_pairs={{0,24},{1,25},{2,26},{3,27},{4,28},{5,29},{6,30},{7,31},{8,0},{9,1... | collective-permute-start | bytes 1572872 | tf_op jit(solution)/shard_map/ppermute | solution.py:40
  104.4 23.1 %collective-permute-start.20 = (bf16[512,512]{1,0:T(8,128)(2,1)}, bf16[512,512]{1,0:T(8,128)(2,1)S(1)}, u32[]{:S(2)}, u32[]{:S(2)}) collective-permute-start(bf16[512,512]{1,0:T(8,128)(2,1)} %collective-permute-done.15.rest_2_), channel_id=1, source_target_pairs={{0,3},{1,0},{2,1},{3,2},{4,7},{5,4},{6,5},{7,6},{8,11},{9,8},{10,9... | collective-permute-start | bytes 1572872 | tf_op jit(solution)/shard_map/ppermute | solution.py:40
  117.2 17.3 %collective-permute-start.25 = (bf16[512,512]{1,0:T(8,128)(2,1)S(1)}, bf16[512,512]{1,0:T(8,128)(2,1)S(1)}, u32[]{:S(2)}, u32[]{:S(2)}) collective-permute-start(bf16[512,512]{1,0:T(8,128)(2,1)S(1)} %collective-permute-done.22.rest_1_), channel_id=1, source_target_pairs={{0,24},{1,25},{2,26},{3,27},{4,28},{5,29},{6,30},{7,31},{8,0},{9,1... | collective-permute-start | bytes 1572872 | tf_op jit(solution)/shard_map/ppermute | solution.py:40
  119.8 14.8 %collective-permute-start.33 = (bf16[512,512]{1,0:T(8,128)(2,1)S(1)}, bf16[512,512]{1,0:T(8,128)(2,1)S(1)}, u32[]{:S(2)}, u32[]{:S(2)}) collective-permute-start(bf16[512,512]{1,0:T(8,128)(2,1)S(1)} %collective-permute-done.19.rest_3_), channel_id=1, source_target_pairs={{0,3},{1,0},{2,1},{3,2},{4,7},{5,4},{6,5},{7,6},{8,11},{9,8},{10,9... | collective-permute-start | bytes 1572872 | tf_op jit(solution)/shard_map/ppermute | solution.py:40
  120.1 14.5 %collective-permute-start.32 = (bf16[512,512]{1,0:T(8,128)(2,1)}, bf16[512,512]{1,0:T(8,128)(2,1)S(1)}, u32[]{:S(2)}, u32[]{:S(2)}) collective-permute-start(bf16[512,512]{1,0:T(8,128)(2,1)} %collective-permute-done.29.rest_2_), channel_id=1, source_target_pairs={{0,1},{1,2},{2,3},{3,0},{4,5},{5,6},{6,7},{7,4},{8,9},{9,10},{10,1... | collective-permute-start | bytes 1572872 | tf_op jit(solution)/shard_map/ppermute | solution.py:40
  127.6 18.3 %collective-permute-start.21 = (bf16[128,512]{1,0:T(8,128)(2,1)S(1)}, bf16[128,512]{1,0:T(8,128)(2,1)S(1)}, u32[]{:S(2)}, u32[]{:S(2)}) collective-permute-start(bf16[128,512]{1,0:T(8,128)(2,1)S(1)} %get-tuple-element.99), channel_id=1, source_target_pairs={{0,8},{1,9},{2,10},{3,11},{4,12},{5,13},{6,14},{7,15},{8,16},{9,17... | collective-permute-start | bytes 393224 | tf_op jit(solution)/shard_map/ppermute | solution.py:40
  127.8 18.1 %collective-permute-start.28 = (bf16[128,512]{1,0:T(8,128)(2,1)S(1)}, bf16[128,512]{1,0:T(8,128)(2,1)S(1)}, u32[]{:S(2)}, u32[]{:S(2)}) collective-permute-start(bf16[128,512]{1,0:T(8,128)(2,1)S(1)} %get-tuple-element.108), channel_id=1, source_target_pairs={{0,24},{1,25},{2,26},{3,27},{4,28},{5,29},{6,30},{7,31},{8,0},{9,1... | collective-permute-start | bytes 393224 | tf_op jit(solution)/shard_map/ppermute | solution.py:40
  (34 other events, 497.1 us)
Sparse Core Ops, SparseCore 0:
  10.2 41.6 all-gather.2
  77.2 42.3 reduce-scatter.1

commit v2 on v1

--- a/solution.py
+++ b/solution.py
@@ -189,10 +189,7 @@
 def input_kernel(parts, last, n_acc, pos_ref, inv_ref, cot_ref, tokv_ref, *rest):
     accs, ghs = rest[:n_acc], rest[n_acc : 2 * n_acc]
     pieces = rest[2 * n_acc : 2 * n_acc + len(last)]
-    out_ref, outv, ghv, acc, wbuf, sem_in, sem_out = rest[2 * n_acc + len(last) :]
-    copies = [pltpu.make_async_copy(p, wbuf.at[k], sem_in.at[k]) for k, p in enumerate(pieces)]
-    for copy in copies:
-        copy.start()
+    out_ref, outv, ghv, acc, sem_out = rest[2 * n_acc + len(last) :]
     total = accs[0][...]
     for a in accs[1:]:
         total = total + a[...]
@@ -203,8 +200,7 @@
             at = (i * 4 + near) * LANE
             ghv[:, at : at + LANE] = p
 
-        copies[i].wait()
-        acc[...] = product(pos_ref, cot_ref, tokv_ref, wbuf[i], which, store, acc[...])
+        acc[...] = product(pos_ref, cot_ref, tokv_ref, pieces[i][...], which, store, acc[...])
     sources = []
     for g, group in zip((*ghs, ghv), (*parts, last), strict=True):
         for i, which in enumerate(group):
@@ -245,15 +241,13 @@
 def input_gradient(pos, inv, cot, tokv, accs, ghs, parts, last, pieces):
     return pl.pallas_call(
         functools.partial(input_kernel, parts, last, len(accs)),
-        in_specs=[SMEM] + [VMEM] * (3 + 2 * len(accs)) + [HBM] * len(last),
+        in_specs=[SMEM] + [VMEM] * (3 + 2 * len(accs) + len(last)),
         out_specs=HBM,
         out_shape=jax.ShapeDtypeStruct((TOK, D), jnp.bfloat16),
         scratch_shapes=[
             pltpu.VMEM((2, TILE, D), jnp.bfloat16),
             pltpu.VMEM((TOK, HALF * len(last)), jnp.bfloat16),
             pltpu.VMEM((TOK, LANE), jnp.float32),
-            pltpu.VMEM((len(last), HALF, KV), jnp.bfloat16),
-            pltpu.SemaphoreType.DMA((len(last),)),
             pltpu.SemaphoreType.DMA((2,)),
         ],
         compiler_params=pltpu.CompilerParams(vmem_limit_bytes=20 * MIB),
@@ -261,7 +255,7 @@
             flops=TOK * KV * D, bytes_accessed=24 * MIB, transcendentals=0
         ),
         name="input_gradient",
-    )(pos, inv, cot, tokv, *accs, *ghs, *[in_hbm(p) for p in pieces])
+    )(pos, inv, cot, tokv, *accs, *ghs, *pieces)
 
 
 def sum_kernel(plan, n_in, *refs):
@@ -374,7 +368,9 @@
     ma0 = q.send(ga30, -1, 0, 0)
     pb1 = q.send(gb11, 0, 0, 1)
     mb0 = q.send(gb30, 0, 0, -1)
-    mine = outer_grad[0].astype(bf16)
+    own = [(0, 0, 0), (0, 0, 1), (1, 0, 0), (1, 0, 1)]
+    gh1, acc1 = gradh(pos, cot, tokv, own, [all_a, near_b, yb], "gradh_own")
+    mine = after(outer_grad[0].astype(bf16), acc1)
     swapped = q.swap(mine, [(0, 1), (1, 0), (2, 3), (3, 2)])
     pa0 = q.send(add(ga10, ra_p), 1, 0, 0)
     ma1 = q.send(add(ga31, ra_m), -1, 0, 0)
@@ -390,9 +386,7 @@
     wa10 = q.send(a0, -1, 0, 0)
     wb31 = q.send(yb, 0, 0, 1)
     wb10 = q.send(near_b, 0, 0, -1)
-    own = [(0, 0, 0), (0, 0, 1), (1, 0, 0), (1, 0, 1)]
-    gh1, acc1 = gradh(pos, cot, tokv, own, [all_a, near_b, yb], "gradh_own")
-    sb = q.send(after(add(gb01, pb1, mb1), acc1), 0, 1, 0)
+    sb = q.send(add(gb01, pb1, mb1), 0, 1, 0)
     wa30 = q.send(a0, 1, 0, 0)
     wa11 = q.send(a1, -1, 0, 0)
     wb30 = q.send(near_b, 0, 0, 1)

time: 157 us -> 156 us (level)
  waiting for transfers between devices: 33.4 us -> 38.4 us
  local copies, waits for them, and re-layouts: 16.4 us -> 12.4 us
  Pallas kernels: 35.1 us -> 32.9 us
    ppermute x2, waiting for transfers between devices: 0.01 us -> 4.95 us  [swap(): self.got.append(lax.ppermute(self.turn(a), 'island', pairs))]
    unnamed x60 -> x54, local copies, waits for them, and re-layouts: 13.4 us -> 10.7 us
  transfers between devices with their start and end apart: 36 -> 36, of which waited for: 7 -> 8; matrix products, arithmetic and copies ran while one was open for 2% -> 1% of each run, Pallas kernels for 23% -> 21%
where the time goes in v2:
time: 156 us; the launch traced here: 155 us
  starting transfers between devices  52.5 us (34%)
  waiting for transfers between devices  38.4 us (25%)
  Pallas kernels  32.9 us (21%)
  between operations  15.2 us (10%)
  local copies, waits for them, and re-layouts  12.4 us (8%)
  other arithmetic  3.62 us (2%)
    ppermute x32, starting transfers between devices, shift(): return lax.ppermute(a, 'fsdp', pairs)  49.3 us
    ppermute x32, waiting for transfers between devices, shift(): return lax.ppermute(a, 'fsdp', pairs)  33.4 us
    pallas_call x3, Pallas kernels, gradh(): pl.pallas_call(functools.partial(gradh_kernel, parts, len(pieces)), in_sp...  10.9 us
    unnamed x54, local copies, waits for them, and re-layouts  10.7 us
    pallas_call x1, Pallas kernels, input_gradient(): pl.pallas_call(functools.partial(input_kernel, parts, last, len(accs)), i...  8.72 us
    pallas_call x3, Pallas kernels, grad_terms(): pl.pallas_call(functools.partial(grad_kernel, parts), in_specs=[SMEM, VME...  6.65 us
    ppermute x2, waiting for transfers between devices, swap(): self.got.append(lax.ppermute(self.turn(a), 'island', pairs))  4.95 us
    pallas_call x9, Pallas kernels, sums(): pl.pallas_call(functools.partial(sum_kernel, plan, len(arrays)), in_specs...  3.49 us
  transfers between devices with their start and end apart: 36, of which 8 were waited for; matrix products, arithmetic and copies ran while one was open for 1% of the time, Pallas kernels for 21%

profile of v2, /device:TPU:0, one launch (start us, length us, event | category | flops | bytes accessed | tf_op | source)
XLA Modules:
  0.0 155.0 jit_solution(1306035798186935095)
XLA Ops:
  8.9 2.9 %collective-permute-start = (bf16[128,512]{1,0:T(8,128)(2,1)S(1)}, bf16[128,512]{1,0:T(8,128)(2,1)S(1)}, u32[]{:S(2)}, u32[]{:S(2)}) collective-permute-start(bf16[128,512]{1,0:T(8,128)(2,1)S(1)} %get-tuple-element.128.refs_0_), channel_id=1, source_target_pairs={{0,24},{1,25},{2,26},{3,27},{4,28},{5,29},{6,30},{7,31},{8,0},{9,1... | collective-permute-start | bytes 393224 | tf_op jit(solution)/shard_map/ppermute | solution.py:40
  14.6 3.4 %copy-done.4 = bf16[1,512,8192]{2,1,0:T(8,128)(2,1)S(1)} copy-done((bf16[1,512,8192]{2,1,0:T(8,128)(2,1)S(1)}, bf16[1,512,8192]{2,1,0:T(8,128)(2,1)}, u32[]{:S(2)}) %copy-start.4) | copy-done | bytes 8388632
  17.9 3.2 %token_stats.1 = (bf16[512,8192]{1,0:T(8,128)(2,1)S(1)}, f32[512,128]{1,0:T(8,128)S(1)}, bf16[512,512]{1,0:T(8,128)(2,1)S(1)}) custom-call(bf16[512,8192]{1,0:T(8,128)(2,1)S(1)} %bitcast.27, bf16[512,512]{1,0:T(8,128)(2,1)S(1)} %bitcast.22), custom_call_target="tpu_custom_call" | custom-call | flops 12582912 | bytes 10485760 | tf_op jit(solution)/shard_map/token_stats/pallas_call | solution.py:87
  22.0 1.8 %grad_far.1 = (bf16[512,512]{1,0:T(8,128)(2,1)S(1)}, bf16[512,512]{1,0:T(8,128)(2,1)S(1)}, bf16[512,512]{1,0:T(8,128)(2,1)S(1)}, bf16[512,512]{1,0:T(8,128)(2,1)S(1)}) custom-call(s32[3]{0:T(128)S(1)} %pad_add_fusion.pos_ref, bf16[512,8192]{1,0:T(8,128)(2,1)S(1)} %get-tuple-element.63.tokv_ref, bf16[512,512]{1,0:T(8,128)(2,1)S(1)} %get-tuple-element.65.cots_ref), custom_call_target="tpu_custom_call" | custom-call | flops 1073741824 | bytes 4194304 | tf_op jit(solution)/shard_map/grad_far/pallas_call | solution.py:116
  23.8 2.0 %collective-permute-start.9 = (bf16[512,512]{1,0:T(8,128)(2,1)S(1)}, bf16[512,512]{1,0:T(8,128)(2,1)S(1)}, u32[]{:S(2)}, u32[]{:S(2)}) collective-permute-start(bf16[512,512]{1,0:T(8,128)(2,1)S(1)} %get-tuple-element.80), channel_id=1, source_target_pairs={{0,1},{1,2},{2,3},{3,0},{4,5},{5,6},{6,7},{7,4},{8,9},{9,10},{10,1... | collective-permute-start | bytes 1572872 | tf_op jit(solution)/shard_map/ppermute | solution.py:40
  25.8 1.8 %collective-permute-start.3 = (bf16[512,512]{1,0:T(8,128)(2,1)S(1)}, bf16[512,512]{1,0:T(8,128)(2,1)S(1)}, u32[]{:S(2)}, u32[]{:S(2)}) collective-permute-start(bf16[512,512]{1,0:T(8,128)(2,1)S(1)} %get-tuple-element.68), channel_id=1, source_target_pairs={{0,8},{1,9},{2,10},{3,11},{4,12},{5,13},{6,14},{7,15},{8,16},{9,17... | collective-permute-start | bytes 1572872 | tf_op jit(solution)/shard_map/ppermute | solution.py:40
  29.1 2.2 %collective-permute-start.12 = (bf16[512,512]{1,0:T(8,128)(2,1)S(1)}, bf16[512,512]{1,0:T(8,128)(2,1)S(1)}, u32[]{:S(2)}, u32[]{:S(2)}) collective-permute-start(bf16[512,512]{1,0:T(8,128)(2,1)S(1)} %get-tuple-element.85), channel_id=1, source_target_pairs={{0,3},{1,0},{2,1},{3,2},{4,7},{5,4},{6,5},{7,6},{8,11},{9,8},{10,9... | collective-permute-start | bytes 1572872 | tf_op jit(solution)/shard_map/ppermute | solution.py:40
  31.3 3.0 %grad_next.1 = (bf16[512,512]{1,0:T(8,128)(2,1)S(1)}, bf16[512,512]{1,0:T(8,128)(2,1)S(1)}, bf16[512,512]{1,0:T(8,128)(2,1)S(1)}, bf16[512,512]{1,0:T(8,128)(2,1...) custom-call(s32[3]{0:T(128)S(1)} %pad_add_fusion.pos_ref, ...), custom_call_target="tpu_custom_call" | custom-call | flops 2147483648 | bytes 8388608 | tf_op jit(solution)/shard_map/grad_next/pallas_call | solution.py:116
  34.2 12.5 %collective-permute-done.9.refs_1_ = bf16[512,512]{1,0:T(8,128)(2,1)S(1)} collective-permute-done((bf16[512,512]{1,0:T(8,128)(2,1)S(1)}, bf16[512,512]{1,0:T(8,128)(2,1)S(1)}, u32[]{:S(2)}, u32[]{:S(2)}) %collective-permute-start.9) | collective-permute-done | bytes 524320 | tf_op jit(solution)/shard_map/ppermute | solution.py:40
  46.8 1.7 %collective-permute-start.4 = (bf16[512,512]{1,0:T(8,128)(2,1)S(1)}, bf16[512,512]{1,0:T(8,128)(2,1)S(1)}, u32[]{:S(2)}, u32[]{:S(2)}) collective-permute-start(bf16[512,512]{1,0:T(8,128)(2,1)S(1)} %get-tuple-element.70), channel_id=1, source_target_pairs={{0,8},{1,9},{2,10},{3,11},{4,12},{5,13},{6,14},{7,15},{8,16},{9,17... | collective-permute-start | bytes 1572872 | tf_op jit(solution)/shard_map/ppermute | solution.py:40
  51.2 3.2 %collective-permute-start.13 = (bf16[512,512]{1,0:T(8,128)(2,1)S(1)}, bf16[512,512]{1,0:T(8,128)(2,1)S(1)}, u32[]{:S(2)}, u32[]{:S(2)}) collective-permute-start(bf16[512,512]{1,0:T(8,128)(2,1)S(1)} %get-tuple-element.86), channel_id=1, source_target_pairs={{0,3},{1,0},{2,1},{3,2},{4,7},{5,4},{6,5},{7,6},{8,11},{9,8},{10,9... | collective-permute-start | bytes 1572872 | tf_op jit(solution)/shard_map/ppermute | solution.py:40
  54.8 6.4 %collective-permute-done.10.refs_1_ = bf16[512,512]{1,0:T(8,128)(2,1)S(1)} collective-permute-done((bf16[512,512]{1,0:T(8,128)(2,1)S(1)}, bf16[512,512]{1,0:T(8,128)(2,1)S(1)}, u32[]{:S(2)}, u32[]{:S(2)}) %collective-permute-start.10) | collective-permute-done | bytes 524320 | tf_op jit(solution)/shard_map/ppermute | solution.py:40
  63.5 1.8 %collective-permute-start.8 = (bf16[512,512]{1,0:T(8,128)(2,1)S(1)}, bf16[512,512]{1,0:T(8,128)(2,1)S(1)}, u32[]{:S(2)}, u32[]{:S(2)}) collective-permute-start(bf16[512,512]{1,0:T(8,128)(2,1)S(1)} %sum_terms.11), channel_id=1, source_target_pairs={{0,24},{1,25},{2,26},{3,27},{4,28},{5,29},{6,30},{7,31},{8,0},{9,1... | collective-permute-start | bytes 1572872 | tf_op jit(solution)/shard_map/ppermute | solution.py:40
  65.4 1.8 %grad_own.1 = (bf16[512,512]{1,0:T(8,128)(2,1)S(1)}, bf16[512,512]{1,0:T(8,128)(2,1)S(1)}, bf16[512,512]{1,0:T(8,128)(2,1)S(1)}, bf16[512,512]{1,0:T(8,128)(2,1)S(1)}) custom-call(s32[3]{0:T(128)S(1)} %pad_add_fusion.pos_ref, bf16[512,8192]{1,0:T(8,128)(2,1)S(1)} %get-tuple-element.63.tokv_ref, bf16[512,512]{1,0:T(8,128)(2,1)S(1)} %get-tuple-element.65.cots_ref), custom_call_target="tpu_custom_call" | custom-call | flops 1073741824 | bytes 4194304 | tf_op jit(solution)/shard_map/grad_own/pallas_call | solution.py:116
  68.2 3.3 %collective-permute-start.14 = (bf16[512,512]{1,0:T(8,128)(2,1)S(1)}, bf16[512,512]{1,0:T(8,128)(2,1)}, u32[]{:S(2)}, u32[]{:S(2)}) collective-permute-start(bf16[512,512]{1,0:T(8,128)(2,1)S(1)} %sum_terms.14), channel_id=1, source_target_pairs={{0,3},{1,0},{2,1},{3,2},{4,7},{5,4},{6,5},{7,6},{8,11},{9,8},{10,9... | collective-permute-start | bytes 1572872 | tf_op jit(solution)/shard_map/ppermute | solution.py:40
  71.5 4.2 %collective-permute-done.11.refs_1_ = bf16[512,512]{1,0:T(8,128)(2,1)S(1)} collective-permute-done((bf16[512,512]{1,0:T(8,128)(2,1)S(1)}, bf16[512,512]{1,0:T(8,128)(2,1)S(1)}, u32[]{:S(2)}, u32[]{:S(2)}) %collective-permute-start.11) | collective-permute-done | bytes 524320 | tf_op jit(solution)/shard_map/ppermute | solution.py:40
  77.2 3.4 %copy-done.1 = bf16[512,8192]{1,0:T(8,128)(2,1)S(1)} copy-done((bf16[512,8192]{1,0:T(8,128)(2,1)S(1)}, bf16[512,8192]{1,0:T(8,128)(2,1)}, u32[]{:S(2)}) %copy-start.1) | copy-done | bytes 8388632
  80.6 3.8 %gradh_own.1 = (bf16[512,2048]{1,0:T(8,128)(2,1)S(1)}, f32[512,128]{1,0:T(8,128)S(1)}) custom-call(s32[3]{0:T(128)S(1)} %pad_add_fusion.pos_ref, bf16[512,512]{1,0:T(8,128)(2,1)S(1)} %bitcast.23, bf16[512,8192]{1,0:T(8,128)(2,1)S(1)} %copy-done.1, bf16[1024,512]{1,0:T(8,128)(2,1)} %bitcast.29, bf16[512,512]{1,0:T(8,128)(2,1)} %copy-done.5, ...), custom_call_target="tpu_custom_call" | custom-call | flops 1073741824 | bytes 4194304 | tf_op jit(solution)/shard_map/gradh_own/pallas_call | solution.py:166
  85.9 2.0 %collective-permute-start.22 = (bf16[512,512]{1,0:T(8,128)(2,1)S(1)}, bf16[512,512]{1,0:T(8,128)(2,1)S(1)}, u32[]{:S(2)}, u32[]{:S(2)}) collective-permute-start(bf16[512,512]{1,0:T(8,128)(2,1)S(1)} %get-tuple-element.103), channel_id=1, source_target_pairs={{0,24},{1,25},{2,26},{3,27},{4,28},{5,29},{6,30},{7,31},{8,0},{9,1... | collective-permute-start | bytes 1572872 | tf_op jit(solution)/shard_map/ppermute | solution.py:40
  88.0 3.0 %collective-permute-start.17 = (bf16[256,512]{1,0:T(8,128)(2,1)S(1)}, bf16[256,512]{1,0:T(8,128)(2,1)S(1)}, u32[]{:S(2)}, u32[]{:S(2)}) collective-permute-start(bf16[256,512]{1,0:T(8,128)(2,1)S(1)} %sum_terms.16), channel_id=1, source_target_pairs={{0,64},{64,0},{32,96},{96,32},{1,65},{65,1},{33,97},{97,33},{2,66}... | collective-permute-start | bytes 786440 | tf_op jit(solution)/shard_map/ppermute | solution.py:317
  91.0 3.1 %collective-permute-start.19 = (bf16[512,512]{1,0:T(8,128)(2,1)S(1)}, bf16[512,512]{1,0:T(8,128)(2,1)S(1)}, u32[]{:S(2)}, u32[]{:S(2)}) collective-permute-start(bf16[512,512]{1,0:T(8,128)(2,1)S(1)} %copy-done.6), channel_id=1, source_target_pairs={{0,3},{1,0},{2,1},{3,2},{4,7},{5,4},{6,5},{7,6},{8,11},{9,8},{10,9... | collective-permute-start | bytes 1572872 | tf_op jit(solution)/shard_map/ppermute | solution.py:40
  95.4 5.0 %collective-permute-done.17 = bf16[256,512]{1,0:T(8,128)(2,1)S(1)} collective-permute-done((bf16[256,512]{1,0:T(8,128)(2,1)S(1)}, bf16[256,512]{1,0:T(8,128)(2,1)S(1)}, u32[]{:S(2)}, u32[]{:S(2)}) %collective-permute-start.17) | collective-permute-done | bytes 262176 | tf_op jit(solution)/shard_map/ppermute | solution.py:317
  101.3 3.2 %collective-permute-start.30 = (bf16[512,512]{1,0:T(8,128)(2,1)S(1)}, bf16[512,512]{1,0:T(8,128)(2,1)S(1)}, u32[]{:S(2)}, u32[]{:S(2)}) collective-permute-start(bf16[512,512]{1,0:T(8,128)(2,1)S(1)} %get-tuple-element.112), channel_id=1, source_target_pairs={{0,24},{1,25},{2,26},{3,27},{4,28},{5,29},{6,30},{7,31},{8,0},{9,1... | collective-permute-start | bytes 1572872 | tf_op jit(solution)/shard_map/ppermute | solution.py:40
  104.5 6.6 %collective-permute-done.19.rest_3_ = bf16[512,512]{1,0:T(8,128)(2,1)S(1)} collective-permute-done((bf16[512,512]{1,0:T(8,128)(2,1)S(1)}, bf16[512,512]{1,0:T(8,128)(2,1)S(1)}, u32[]{:S(2)}, u32[]{:S(2)}) %collective-permute-start.19) | collective-permute-done | bytes 524320 | tf_op jit(solution)/shard_map/ppermute | solution.py:40
  111.1 3.7 %collective-permute-start.20 = (bf16[512,512]{1,0:T(8,128)(2,1)}, bf16[512,512]{1,0:T(8,128)(2,1)S(1)}, u32[]{:S(2)}, u32[]{:S(2)}) collective-permute-start(bf16[512,512]{1,0:T(8,128)(2,1)} %collective-permute-done.15.rest_2_), channel_id=1, source_target_pairs={{0,3},{1,0},{2,1},{3,2},{4,7},{5,4},{6,5},{7,6},{8,11},{9,8},{10,9... | collective-permute-start | bytes 1572872 | tf_op jit(solution)/shard_map/ppermute | solution.py:40
  115.8 2.2 %collective-permute-done.18.refs_3_ = bf16[512,512]{1,0:T(8,128)(2,1)S(1)} collective-permute-done((bf16[512,512]{1,0:T(8,128)(2,1)S(1)}, bf16[512,512]{1,0:T(8,128)(2,1)S(1)}, u32[]{:S(2)}, u32[]{:S(2)}) %collective-permute-start.18) | collective-permute-done | bytes 524320 | tf_op jit(solution)/shard_map/ppermute | solution.py:40
  118.7 2.5 %collective-permute-start.25 = (bf16[512,512]{1,0:T(8,128)(2,1)S(1)}, bf16[512,512]{1,0:T(8,128)(2,1)S(1)}, u32[]{:S(2)}, u32[]{:S(2)}) collective-permute-start(bf16[512,512]{1,0:T(8,128)(2,1)S(1)} %collective-permute-done.22.rest_1_), channel_id=1, source_target_pairs={{0,24},{1,25},{2,26},{3,27},{4,28},{5,29},{6,30},{7,31},{8,0},{9,1... | collective-permute-start | bytes 1572872 | tf_op jit(solution)/shard_map/ppermute | solution.py:40
  121.2 2.5 %collective-permute-start.33 = (bf16[512,512]{1,0:T(8,128)(2,1)S(1)}, bf16[512,512]{1,0:T(8,128)(2,1)S(1)}, u32[]{:S(2)}, u32[]{:S(2)}) collective-permute-start(bf16[512,512]{1,0:T(8,128)(2,1)S(1)} %collective-permute-done.19.rest_3_), channel_id=1, source_target_pairs={{0,3},{1,0},{2,1},{3,2},{4,7},{5,4},{6,5},{7,6},{8,11},{9,8},{10,9... | collective-permute-start | bytes 1572872 | tf_op jit(solution)/shard_map/ppermute | solution.py:40
  125.7 3.5 %gradh_one.1 = (bf16[512,2048]{1,0:T(8,128)(2,1)S(1)}, f32[512,128]{1,0:T(8,128)S(1)}) custom-call(s32[3]{0:T(128)S(1)} %pad_add_fusion.pos_ref, bf16[512,512]{1,0:T(8,128)(2,1)S(1)} %bitcast.24, bf16[512,8192]{1,0:T(8,128)(2,1)S(1)} %copy-done.1, bf16[512,512]{1,0:T(8,128)(2,1)} %copy-done.18, bf16[512,512]{1,0:T(8,128)(2,1)} %copy-done.17, ...), custom_call_target="tpu_custom_call" | custom-call | flops 1073741824 | bytes 4194304 | tf_op jit(solution)/shard_map/gradh_one/pallas_call | solution.py:166
  130.3 3.5 %gradh_two.1 = (bf16[512,2048]{1,0:T(8,128)(2,1)S(1)}, f32[512,128]{1,0:T(8,128)S(1)}) custom-call(s32[3]{0:T(128)S(1)} %pad_add_fusion.pos_ref, bf16[512,512]{1,0:T(8,128)(2,1)S(1)} %bitcast.25, bf16[512,8192]{1,0:T(8,128)(2,1)S(1)} %copy-done.1, bf16[512,512]{1,0:T(8,128)(2,1)} %copy-done.21, bf16[512,512]{1,0:T(8,128)(2,1)} %copy-done.22, ...), custom_call_target="tpu_custom_call" | custom-call | flops 1073741824 | bytes 4194304 | tf_op jit(solution)/shard_map/gradh_two/pallas_call | solution.py:166
  133.9 2.8 %collective-permute-start.28 = (bf16[128,512]{1,0:T(8,128)(2,1)S(1)}, bf16[128,512]{1,0:T(8,128)(2,1)S(1)}, u32[]{:S(2)}, u32[]{:S(2)}) collective-permute-start(bf16[128,512]{1,0:T(8,128)(2,1)S(1)} %get-tuple-element.108), channel_id=1, source_target_pairs={{0,24},{1,25},{2,26},{3,27},{4,28},{5,29},{6,30},{7,31},{8,0},{9,1... | collective-permute-start | bytes 393224 | tf_op jit(solution)/shard_map/ppermute | solution.py:40
  137.0 8.7 %input_gradient.1 = bf16[512,8192]{1,0:T(8,128)(2,1)} custom-call(s32[3]{0:T(128)S(1)} %pad_add_fusion.pos_ref, f32[512,128]{1,0:T(8,128)S(1)} %copy-done.12, bf16[512,512]{1,0:T(8,128)(2,1)S(1)} %bitcast.26, bf16[512,8192]{1,0:T(8,128)(2,1)S(1)} %copy-done.1, f32[512,128]{1,0:T(8,128)S(1)} %get-tuple-element.90.rest_0_, ...), custom_call_target="tpu_custom_call" | custom-call | flops 2147483648 | bytes 25165824 | tf_op jit(solution)/shard_map/input_gradient/pallas_call | solution.py:242
  (121 shorter events, 24.9 us)
Async XLA Ops:
  7.2 70.0 %all-gather.3.cloned.1.call-start = ((), (), s32[]{:S(2)}) async-start(), calls=%async_computation.2 | async-start | bytes 1179648 | tf_op jit(solution)/shard_map/all_gather | solution.py:339
  8.9 137.0 %reduce-scatter.2.cloned.1.call-start = ((), (), s32[]{:S(2)}) async-start(), calls=%async_computation.1 | async-start | bytes 1179648 | tf_op jit(solution)/shard_map/reduce_scatter | solution.py:399
  8.9 13.0 %collective-permute-start = (bf16[128,512]{1,0:T(8,128)(2,1)S(1)}, bf16[128,512]{1,0:T(8,128)(2,1)S(1)}, u32[]{:S(2)}, u32[]{:S(2)}) collective-permute-start(bf16[128,512]{1,0:T(8,128)(2,1)S(1)} %get-tuple-element.128.refs_0_), channel_id=1, source_target_pairs={{0,24},{1,25},{2,26},{3,27},{4,28},{5,29},{6,30},{7,31},{8,0},{9,1... | collective-permute-start | bytes 393224 | tf_op jit(solution)/shard_map/ppermute | solution.py:40
  23.8 22.9 %collective-permute-start.9 = (bf16[512,512]{1,0:T(8,128)(2,1)S(1)}, bf16[512,512]{1,0:T(8,128)(2,1)S(1)}, u32[]{:S(2)}, u32[]{:S(2)}) collective-permute-start(bf16[512,512]{1,0:T(8,128)(2,1)S(1)} %get-tuple-element.80), channel_id=1, source_target_pairs={{0,1},{1,2},{2,3},{3,0},{4,5},{5,6},{6,7},{7,4},{8,9},{9,10},{10,1... | collective-permute-start | bytes 1572872 | tf_op jit(solution)/shard_map/ppermute | solution.py:40
  25.8 20.9 %collective-permute-start.3 = (bf16[512,512]{1,0:T(8,128)(2,1)S(1)}, bf16[512,512]{1,0:T(8,128)(2,1)S(1)}, u32[]{:S(2)}, u32[]{:S(2)}) collective-permute-start(bf16[512,512]{1,0:T(8,128)(2,1)S(1)} %get-tuple-element.68), channel_id=1, source_target_pairs={{0,8},{1,9},{2,10},{3,11},{4,12},{5,13},{6,14},{7,15},{8,16},{9,17... | collective-permute-start | bytes 1572872 | tf_op jit(solution)/shard_map/ppermute | solution.py:40
  27.6 20.8 %collective-permute-start.6 = (bf16[512,512]{1,0:T(8,128)(2,1)S(1)}, bf16[512,512]{1,0:T(8,128)(2,1)S(1)}, u32[]{:S(2)}, u32[]{:S(2)}) collective-permute-start(bf16[512,512]{1,0:T(8,128)(2,1)S(1)} %get-tuple-element.73), channel_id=1, source_target_pairs={{0,24},{1,25},{2,26},{3,27},{4,28},{5,29},{6,30},{7,31},{8,0},{9,1... | collective-permute-start | bytes 1572872 | tf_op jit(solution)/shard_map/ppermute | solution.py:40
  29.1 22.1 %collective-permute-start.12 = (bf16[512,512]{1,0:T(8,128)(2,1)S(1)}, bf16[512,512]{1,0:T(8,128)(2,1)S(1)}, u32[]{:S(2)}, u32[]{:S(2)}) collective-permute-start(bf16[512,512]{1,0:T(8,128)(2,1)S(1)} %get-tuple-element.85), channel_id=1, source_target_pairs={{0,3},{1,0},{2,1},{3,2},{4,7},{5,4},{6,5},{7,6},{8,11},{9,8},{10,9... | collective-permute-start | bytes 1572872 | tf_op jit(solution)/shard_map/ppermute | solution.py:40
  46.7 14.5 %collective-permute-start.10 = (bf16[512,512]{1,0:T(8,128)(2,1)S(1)}, bf16[512,512]{1,0:T(8,128)(2,1)S(1)}, u32[]{:S(2)}, u32[]{:S(2)}) collective-permute-start(bf16[512,512]{1,0:T(8,128)(2,1)S(1)} %get-tuple-element.82), channel_id=1, source_target_pairs={{0,1},{1,2},{2,3},{3,0},{4,5},{5,6},{6,7},{7,4},{8,9},{9,10},{10,1... | collective-permute-start | bytes 1572872 | tf_op jit(solution)/shard_map/ppermute | solution.py:40
  46.8 15.3 %collective-permute-start.4 = (bf16[512,512]{1,0:T(8,128)(2,1)S(1)}, bf16[512,512]{1,0:T(8,128)(2,1)S(1)}, u32[]{:S(2)}, u32[]{:S(2)}) collective-permute-start(bf16[512,512]{1,0:T(8,128)(2,1)S(1)} %get-tuple-element.70), channel_id=1, source_target_pairs={{0,8},{1,9},{2,10},{3,11},{4,12},{5,13},{6,14},{7,15},{8,16},{9,17... | collective-permute-start | bytes 1572872 | tf_op jit(solution)/shard_map/ppermute | solution.py:40
  48.4 15.1 %collective-permute-start.7 = (bf16[512,512]{1,0:T(8,128)(2,1)S(1)}, bf16[512,512]{1,0:T(8,128)(2,1)S(1)}, u32[]{:S(2)}, u32[]{:S(2)}) collective-permute-start(bf16[512,512]{1,0:T(8,128)(2,1)S(1)} %get-tuple-element.74), channel_id=1, source_target_pairs={{0,24},{1,25},{2,26},{3,27},{4,28},{5,29},{6,30},{7,31},{8,0},{9,1... | collective-permute-start | bytes 1572872 | tf_op jit(solution)/shard_map/ppermute | solution.py:40
  50.0 21.5 %collective-permute-start.15 = (bf16[512,512]{1,0:T(8,128)(2,1)S(1)}, bf16[512,512]{1,0:T(8,128)(2,1)}, u32[]{:S(2)}, u32[]{:S(2)}) collective-permute-start(bf16[512,512]{1,0:T(8,128)(2,1)S(1)} %sum_terms.9.rest_1_), channel_id=1, source_target_pairs={{0,4},{1,5},{2,6},{3,7},{4,0},{5,1},{6,2},{7,3},{8,12},{9,13},{10,... | collective-permute-start | bytes 1572872 | tf_op jit(solution)/shard_map/ppermute | solution.py:40
  51.2 17.0 %collective-permute-start.13 = (bf16[512,512]{1,0:T(8,128)(2,1)S(1)}, bf16[512,512]{1,0:T(8,128)(2,1)S(1)}, u32[]{:S(2)}, u32[]{:S(2)}) collective-permute-start(bf16[512,512]{1,0:T(8,128)(2,1)S(1)} %get-tuple-element.86), channel_id=1, source_target_pairs={{0,3},{1,0},{2,1},{3,2},{4,7},{5,4},{6,5},{7,6},{8,11},{9,8},{10,9... | collective-permute-start | bytes 1572872 | tf_op jit(solution)/shard_map/ppermute | solution.py:40
  62.1 13.6 %collective-permute-start.11 = (bf16[512,512]{1,0:T(8,128)(2,1)S(1)}, bf16[512,512]{1,0:T(8,128)(2,1)S(1)}, u32[]{:S(2)}, u32[]{:S(2)}) collective-permute-start(bf16[512,512]{1,0:T(8,128)(2,1)S(1)} %sum_terms.13), channel_id=1, source_target_pairs={{0,1},{1,2},{2,3},{3,0},{4,5},{5,6},{6,7},{7,4},{8,9},{9,10},{10,1... | collective-permute-start | bytes 1572872 | tf_op jit(solution)/shard_map/ppermute | solution.py:40
  62.1 13.6 %collective-permute-start.5 = (bf16[512,512]{1,0:T(8,128)(2,1)S(1)}, bf16[512,512]{1,0:T(8,128)(2,1)S(1)}, u32[]{:S(2)}, u32[]{:S(2)}) collective-permute-start(bf16[512,512]{1,0:T(8,128)(2,1)S(1)} %sum_terms.10), channel_id=1, source_target_pairs={{0,8},{1,9},{2,10},{3,11},{4,12},{5,13},{6,14},{7,15},{8,16},{9,17... | collective-permute-start | bytes 1572872 | tf_op jit(solution)/shard_map/ppermute | solution.py:40
  63.5 12.2 %collective-permute-start.8 = (bf16[512,512]{1,0:T(8,128)(2,1)S(1)}, bf16[512,512]{1,0:T(8,128)(2,1)S(1)}, u32[]{:S(2)}, u32[]{:S(2)}) collective-permute-start(bf16[512,512]{1,0:T(8,128)(2,1)S(1)} %sum_terms.11), channel_id=1, source_target_pairs={{0,24},{1,25},{2,26},{3,27},{4,28},{5,29},{6,30},{7,31},{8,0},{9,1... | collective-permute-start | bytes 1572872 | tf_op jit(solution)/shard_map/ppermute | solution.py:40
  68.2 22.8 %collective-permute-start.14 = (bf16[512,512]{1,0:T(8,128)(2,1)S(1)}, bf16[512,512]{1,0:T(8,128)(2,1)}, u32[]{:S(2)}, u32[]{:S(2)}) collective-permute-start(bf16[512,512]{1,0:T(8,128)(2,1)S(1)} %sum_terms.14), channel_id=1, source_target_pairs={{0,3},{1,0},{2,1},{3,2},{4,7},{5,4},{6,5},{7,6},{8,11},{9,8},{10,9... | collective-permute-start | bytes 1572872 | tf_op jit(solution)/shard_map/ppermute | solution.py:40
  75.7 19.7 %collective-permute-start.29 = (bf16[512,512]{1,0:T(8,128)(2,1)}, bf16[512,512]{1,0:T(8,128)(2,1)}, u32[]{:S(2)}, u32[]{:S(2)}) collective-permute-start(bf16[512,512]{1,0:T(8,128)(2,1)} %collective-permute-done.15.rest_2_), channel_id=1, source_target_pairs={{0,1},{1,2},{2,3},{3,0},{4,5},{5,6},{6,7},{7,4},{8,9},{9,10},{10,1... | collective-permute-start | bytes 1572872 | tf_op jit(solution)/shard_map/ppermute | solution.py:40
  84.6 16.6 %collective-permute-start.23 = (bf16[512,512]{1,0:T(8,128)(2,1)S(1)}, bf16[512,512]{1,0:T(8,128)(2,1)S(1)}, u32[]{:S(2)}, u32[]{:S(2)}) collective-permute-start(bf16[512,512]{1,0:T(8,128)(2,1)S(1)} %get-tuple-element.112), channel_id=1, source_target_pairs={{0,8},{1,9},{2,10},{3,11},{4,12},{5,13},{6,14},{7,15},{8,16},{9,17... | collective-permute-start | bytes 1572872 | tf_op jit(solution)/shard_map/ppermute | solution.py:40
  85.9 15.4 %collective-permute-start.22 = (bf16[512,512]{1,0:T(8,128)(2,1)S(1)}, bf16[512,512]{1,0:T(8,128)(2,1)S(1)}, u32[]{:S(2)}, u32[]{:S(2)}) collective-permute-start(bf16[512,512]{1,0:T(8,128)(2,1)S(1)} %get-tuple-element.103), channel_id=1, source_target_pairs={{0,24},{1,25},{2,26},{3,27},{4,28},{5,29},{6,30},{7,31},{8,0},{9,1... | collective-permute-start | bytes 1572872 | tf_op jit(solution)/shard_map/ppermute | solution.py:40
  88.0 12.4 %collective-permute-start.17 = (bf16[256,512]{1,0:T(8,128)(2,1)S(1)}, bf16[256,512]{1,0:T(8,128)(2,1)S(1)}, u32[]{:S(2)}, u32[]{:S(2)}) collective-permute-start(bf16[256,512]{1,0:T(8,128)(2,1)S(1)} %sum_terms.16), channel_id=1, source_target_pairs={{0,64},{64,0},{32,96},{96,32},{1,65},{65,1},{33,97},{97,33},{2,66}... | collective-permute-start | bytes 786440 | tf_op jit(solution)/shard_map/ppermute | solution.py:317
  91.0 20.1 %collective-permute-start.19 = (bf16[512,512]{1,0:T(8,128)(2,1)S(1)}, bf16[512,512]{1,0:T(8,128)(2,1)S(1)}, u32[]{:S(2)}, u32[]{:S(2)}) collective-permute-start(bf16[512,512]{1,0:T(8,128)(2,1)S(1)} %copy-done.6), channel_id=1, source_target_pairs={{0,3},{1,0},{2,1},{3,2},{4,7},{5,4},{6,5},{7,6},{8,11},{9,8},{10,9... | collective-permute-start | bytes 1572872 | tf_op jit(solution)/shard_map/ppermute | solution.py:40
  95.3 20.4 %collective-permute-start.31 = (bf16[512,512]{1,0:T(8,128)(2,1)S(1)}, bf16[512,512]{1,0:T(8,128)(2,1)S(1)}, u32[]{:S(2)}, u32[]{:S(2)}) collective-permute-start(bf16[512,512]{1,0:T(8,128)(2,1)S(1)} %copy-done.6), channel_id=1, source_target_pairs={{0,1},{1,2},{2,3},{3,0},{4,5},{5,6},{6,7},{7,4},{8,9},{9,10},{10,1... | collective-permute-start | bytes 1572872 | tf_op jit(solution)/shard_map/ppermute | solution.py:40
  100.4 17.6 %collective-permute-start.18 = (bf16[512,512]{1,0:T(8,128)(2,1)S(1)}, bf16[512,512]{1,0:T(8,128)(2,1)S(1)}, u32[]{:S(2)}, u32[]{:S(2)}) collective-permute-start(bf16[512,512]{1,0:T(8,128)(2,1)S(1)} %sum_terms.15), channel_id=1, source_target_pairs={{0,4},{1,5},{2,6},{3,7},{4,0},{5,1},{6,2},{7,3},{8,12},{9,13},{10,... | collective-permute-start | bytes 1572872 | tf_op jit(solution)/shard_map/ppermute | solution.py:40
  101.3 17.4 %collective-permute-start.24 = (bf16[512,512]{1,0:T(8,128)(2,1)S(1)}, bf16[512,512]{1,0:T(8,128)(2,1)S(1)}, u32[]{:S(2)}, u32[]{:S(2)}) collective-permute-start(bf16[512,512]{1,0:T(8,128)(2,1)S(1)} %get-tuple-element.103), channel_id=1, source_target_pairs={{0,8},{1,9},{2,10},{3,11},{4,12},{5,13},{6,14},{7,15},{8,16},{9,17... | collective-permute-start | bytes 1572872 | tf_op jit(solution)/shard_map/ppermute | solution.py:40
  101.3 22.4 %collective-permute-start.30 = (bf16[512,512]{1,0:T(8,128)(2,1)S(1)}, bf16[512,512]{1,0:T(8,128)(2,1)S(1)}, u32[]{:S(2)}, u32[]{:S(2)}) collective-permute-start(bf16[512,512]{1,0:T(8,128)(2,1)S(1)} %get-tuple-element.112), channel_id=1, source_target_pairs={{0,24},{1,25},{2,26},{3,27},{4,28},{5,29},{6,30},{7,31},{8,0},{9,1... | collective-permute-start | bytes 1572872 | tf_op jit(solution)/shard_map/ppermute | solution.py:40
  111.1 18.4 %collective-permute-start.20 = (bf16[512,512]{1,0:T(8,128)(2,1)}, bf16[512,512]{1,0:T(8,128)(2,1)S(1)}, u32[]{:S(2)}, u32[]{:S(2)}) collective-permute-start(bf16[512,512]{1,0:T(8,128)(2,1)} %collective-permute-done.15.rest_2_), channel_id=1, source_target_pairs={{0,3},{1,0},{2,1},{3,2},{4,7},{5,4},{6,5},{7,6},{8,11},{9,8},{10,9... | collective-permute-start | bytes 1572872 | tf_op jit(solution)/shard_map/ppermute | solution.py:40
  118.0 15.9 %collective-permute-start.27 = (bf16[512,512]{1,0:T(8,128)(2,1)S(1)}, bf16[512,512]{1,0:T(8,128)(2,1)S(1)}, u32[]{:S(2)}, u32[]{:S(2)}) collective-permute-start(bf16[512,512]{1,0:T(8,128)(2,1)S(1)} %collective-permute-done.23.rest_0_), channel_id=1, source_target_pairs={{0,8},{1,9},{2,10},{3,11},{4,12},{5,13},{6,14},{7,15},{8,16},{9,17... | collective-permute-start | bytes 1572872 | tf_op jit(solution)/shard_map/ppermute | solution.py:40
  118.7 18.0 %collective-permute-start.25 = (bf16[512,512]{1,0:T(8,128)(2,1)S(1)}, bf16[512,512]{1,0:T(8,128)(2,1)S(1)}, u32[]{:S(2)}, u32[]{:S(2)}) collective-permute-start(bf16[512,512]{1,0:T(8,128)(2,1)S(1)} %collective-permute-done.22.rest_1_), channel_id=1, source_target_pairs={{0,24},{1,25},{2,26},{3,27},{4,28},{5,29},{6,30},{7,31},{8,0},{9,1... | collective-permute-start | bytes 1572872 | tf_op jit(solution)/shard_map/ppermute | solution.py:40
  121.2 15.8 %collective-permute-start.33 = (bf16[512,512]{1,0:T(8,128)(2,1)S(1)}, bf16[512,512]{1,0:T(8,128)(2,1)S(1)}, u32[]{:S(2)}, u32[]{:S(2)}) collective-permute-start(bf16[512,512]{1,0:T(8,128)(2,1)S(1)} %collective-permute-done.19.rest_3_), channel_id=1, source_target_pairs={{0,3},{1,0},{2,1},{3,2},{4,7},{5,4},{6,5},{7,6},{8,11},{9,8},{10,9... | collective-permute-start | bytes 1572872 | tf_op jit(solution)/shard_map/ppermute | solution.py:40
  123.7 13.3 %collective-permute-start.32 = (bf16[512,512]{1,0:T(8,128)(2,1)}, bf16[512,512]{1,0:T(8,128)(2,1)S(1)}, u32[]{:S(2)}, u32[]{:S(2)}) collective-permute-start(bf16[512,512]{1,0:T(8,128)(2,1)} %collective-permute-done.29.rest_2_), channel_id=1, source_target_pairs={{0,1},{1,2},{2,3},{3,0},{4,5},{5,6},{6,7},{7,4},{8,9},{9,10},{10,1... | collective-permute-start | bytes 1572872 | tf_op jit(solution)/shard_map/ppermute | solution.py:40
  129.5 16.2 %collective-permute-start.21 = (bf16[128,512]{1,0:T(8,128)(2,1)S(1)}, bf16[128,512]{1,0:T(8,128)(2,1)S(1)}, u32[]{:S(2)}, u32[]{:S(2)}) collective-permute-start(bf16[128,512]{1,0:T(8,128)(2,1)S(1)} %get-tuple-element.99), channel_id=1, source_target_pairs={{0,8},{1,9},{2,10},{3,11},{4,12},{5,13},{6,14},{7,15},{8,16},{9,17... | collective-permute-start | bytes 393224 | tf_op jit(solution)/shard_map/ppermute | solution.py:40
  133.9 11.9 %collective-permute-start.28 = (bf16[128,512]{1,0:T(8,128)(2,1)S(1)}, bf16[128,512]{1,0:T(8,128)(2,1)S(1)}, u32[]{:S(2)}, u32[]{:S(2)}) collective-permute-start(bf16[128,512]{1,0:T(8,128)(2,1)S(1)} %get-tuple-element.108), channel_id=1, source_target_pairs={{0,24},{1,25},{2,26},{3,27},{4,28},{5,29},{6,30},{7,31},{8,0},{9,1... | collective-permute-start | bytes 393224 | tf_op jit(solution)/shard_map/ppermute | solution.py:40
  (31 other events, 443.0 us)
Sparse Core Ops, SparseCore 0:
  10.2 41.6 all-gather.2
  77.2 43.4 reduce-scatter.1

commit v3 on v2

--- a/solution.py
+++ b/solution.py
@@ -368,16 +368,16 @@
     ma0 = q.send(ga30, -1, 0, 0)
     pb1 = q.send(gb11, 0, 0, 1)
     mb0 = q.send(gb30, 0, 0, -1)
-    own = [(0, 0, 0), (0, 0, 1), (1, 0, 0), (1, 0, 1)]
-    gh1, acc1 = gradh(pos, cot, tokv, own, [all_a, near_b, yb], "gradh_own")
-    mine = after(outer_grad[0].astype(bf16), acc1)
+    mine = outer_grad[0].astype(bf16)
     swapped = q.swap(mine, [(0, 1), (1, 0), (2, 3), (3, 2)])
     pa0 = q.send(add(ga10, ra_p), 1, 0, 0)
     ma1 = q.send(add(ga31, ra_m), -1, 0, 0)
     pb0 = q.send(add(gb10, rb_p), 0, 0, 1)
     mb1 = q.send(add(gb31, rb_m), 0, 0, -1)
     pair = add(mine, swapped)
-    other = q.swap(pair, [(0, 2), (2, 0), (1, 3), (3, 1)])
+    own = [(0, 0, 0), (0, 0, 1), (1, 0, 0), (1, 0, 1)]
+    gh1, acc1 = gradh(pos, cot, tokv, own, [all_a, near_b, yb], "gradh_own")
+    other = q.swap(after(pair, acc1), [(0, 2), (2, 0), (1, 3), (3, 1)])
     ga00, ga01, gb00, gb01 = grad_terms(
         pos, tokv, cots, [(0, 0, 0), (0, 0, 1), (1, 0, 0), (1, 0, 1)], "grad_own"
     )

time: 156 us -> 154 us (0.987)
  waiting for transfers between devices: 38.4 us -> 35.3 us
    ppermute x32, waiting for transfers between devices: 33.4 us -> 31.3 us  [shift(): return lax.ppermute(a, 'fsdp', pairs)]
    unnamed x54 -> x52, local copies, waits for them, and re-layouts: 10.7 us -> 10.6 us
  transfers between devices with their start and end apart: 36 -> 36, of which waited for: 8 -> 7; matrix products, arithmetic and copies ran while one was open for 1% -> 2% of each run, Pallas kernels for 21% -> 22%
where the time goes in v3:
time: 154 us; the launch traced here: 153 us
  starting transfers between devices  51.4 us (33%)
  waiting for transfers between devices  35.3 us (23%)
  Pallas kernels  33.6 us (22%)
  between operations  15.3 us (10%)
  local copies, waits for them, and re-layouts  13.7 us (9%)
  other arithmetic  3.61 us (2%)
    ppermute x32, starting transfers between devices, shift(): return lax.ppermute(a, 'fsdp', pairs)  48.3 us
    ppermute x32, waiting for transfers between devices, shift(): return lax.ppermute(a, 'fsdp', pairs)  31.3 us
    unnamed x52, local copies, waits for them, and re-layouts  10.6 us
    pallas_call x3, Pallas kernels, gradh(): pl.pallas_call(functools.partial(gradh_kernel, parts, len(pieces)), in_sp...  10.6 us
    pallas_call x1, Pallas kernels, input_gradient(): pl.pallas_call(functools.partial(input_kernel, parts, last, len(accs)), i...  8.72 us
    pallas_call x3, Pallas kernels, grad_terms(): pl.pallas_call(functools.partial(grad_kernel, parts), in_specs=[SMEM, VME...  6.65 us
    pallas_call x9, Pallas kernels, sums(): pl.pallas_call(functools.partial(sum_kernel, plan, len(arrays)), in_specs...  4.44 us
    ppermute x2, waiting for transfers between devices, swap(): self.got.append(lax.ppermute(self.turn(a), 'island', pairs))  3.96 us
  transfers between devices with their start and end apart: 36, of which 7 were waited for; matrix products, arithmetic and copies ran while one was open for 2% of the time, Pallas kernels for 22%

profile of v3, /device:TPU:0, one launch (start us, length us, event | category | flops | bytes accessed | tf_op | source)
XLA Modules:
  0.0 152.9 jit_solution(17821183833301079550)
XLA Ops:
  8.9 2.9 %collective-permute-start = (bf16[128,512]{1,0:T(8,128)(2,1)S(1)}, bf16[128,512]{1,0:T(8,128)(2,1)S(1)}, u32[]{:S(2)}, u32[]{:S(2)}) collective-permute-start(bf16[128,512]{1,0:T(8,128)(2,1)S(1)} %get-tuple-element.128.refs_0_), channel_id=1, source_target_pairs={{0,24},{1,25},{2,26},{3,27},{4,28},{5,29},{6,30},{7,31},{8,0},{9,1... | collective-permute-start | bytes 393224 | tf_op jit(solution)/shard_map/ppermute | solution.py:40
  14.6 3.4 %copy-done.4 = bf16[1,512,8192]{2,1,0:T(8,128)(2,1)S(1)} copy-done((bf16[1,512,8192]{2,1,0:T(8,128)(2,1)S(1)}, bf16[1,512,8192]{2,1,0:T(8,128)(2,1)}, u32[]{:S(2)}) %copy-start.4) | copy-done | bytes 8388632
  17.9 3.2 %token_stats.1 = (bf16[512,8192]{1,0:T(8,128)(2,1)S(1)}, f32[512,128]{1,0:T(8,128)S(1)}, bf16[512,512]{1,0:T(8,128)(2,1)S(1)}) custom-call(bf16[512,8192]{1,0:T(8,128)(2,1)S(1)} %bitcast.27, bf16[512,512]{1,0:T(8,128)(2,1)S(1)} %bitcast.22), custom_call_target="tpu_custom_call" | custom-call | flops 12582912 | bytes 10485760 | tf_op jit(solution)/shard_map/token_stats/pallas_call | solution.py:87
  22.0 1.8 %grad_far.1 = (bf16[512,512]{1,0:T(8,128)(2,1)S(1)}, bf16[512,512]{1,0:T(8,128)(2,1)S(1)}, bf16[512,512]{1,0:T(8,128)(2,1)S(1)}, bf16[512,512]{1,0:T(8,128)(2,1)S(1)}) custom-call(s32[3]{0:T(128)S(1)} %pad_add_fusion.pos_ref, bf16[512,8192]{1,0:T(8,128)(2,1)S(1)} %get-tuple-element.63.tokv_ref, bf16[512,512]{1,0:T(8,128)(2,1)S(1)} %get-tuple-element.65.cots_ref), custom_call_target="tpu_custom_call" | custom-call | flops 1073741824 | bytes 4194304 | tf_op jit(solution)/shard_map/grad_far/pallas_call | solution.py:116
  23.8 2.0 %collective-permute-start.9 = (bf16[512,512]{1,0:T(8,128)(2,1)S(1)}, bf16[512,512]{1,0:T(8,128)(2,1)S(1)}, u32[]{:S(2)}, u32[]{:S(2)}) collective-permute-start(bf16[512,512]{1,0:T(8,128)(2,1)S(1)} %get-tuple-element.80), channel_id=1, source_target_pairs={{0,1},{1,2},{2,3},{3,0},{4,5},{5,6},{6,7},{7,4},{8,9},{9,10},{10,1... | collective-permute-start | bytes 1572872 | tf_op jit(solution)/shard_map/ppermute | solution.py:40
  25.8 1.8 %collective-permute-start.3 = (bf16[512,512]{1,0:T(8,128)(2,1)S(1)}, bf16[512,512]{1,0:T(8,128)(2,1)S(1)}, u32[]{:S(2)}, u32[]{:S(2)}) collective-permute-start(bf16[512,512]{1,0:T(8,128)(2,1)S(1)} %get-tuple-element.68), channel_id=1, source_target_pairs={{0,8},{1,9},{2,10},{3,11},{4,12},{5,13},{6,14},{7,15},{8,16},{9,17... | collective-permute-start | bytes 1572872 | tf_op jit(solution)/shard_map/ppermute | solution.py:40
  29.1 2.2 %collective-permute-start.12 = (bf16[512,512]{1,0:T(8,128)(2,1)S(1)}, bf16[512,512]{1,0:T(8,128)(2,1)S(1)}, u32[]{:S(2)}, u32[]{:S(2)}) collective-permute-start(bf16[512,512]{1,0:T(8,128)(2,1)S(1)} %get-tuple-element.85), channel_id=1, source_target_pairs={{0,3},{1,0},{2,1},{3,2},{4,7},{5,4},{6,5},{7,6},{8,11},{9,8},{10,9... | collective-permute-start | bytes 1572872 | tf_op jit(solution)/shard_map/ppermute | solution.py:40
  31.3 3.0 %grad_next.1 = (bf16[512,512]{1,0:T(8,128)(2,1)S(1)}, bf16[512,512]{1,0:T(8,128)(2,1)S(1)}, bf16[512,512]{1,0:T(8,128)(2,1)S(1)}, bf16[512,512]{1,0:T(8,128)(2,1...) custom-call(s32[3]{0:T(128)S(1)} %pad_add_fusion.pos_ref, ...), custom_call_target="tpu_custom_call" | custom-call | flops 2147483648 | bytes 8388608 | tf_op jit(solution)/shard_map/grad_next/pallas_call | solution.py:116
  34.2 12.5 %collective-permute-done.9.refs_1_ = bf16[512,512]{1,0:T(8,128)(2,1)S(1)} collective-permute-done((bf16[512,512]{1,0:T(8,128)(2,1)S(1)}, bf16[512,512]{1,0:T(8,128)(2,1)S(1)}, u32[]{:S(2)}, u32[]{:S(2)}) %collective-permute-start.9) | collective-permute-done | bytes 524320 | tf_op jit(solution)/shard_map/ppermute | solution.py:40
  46.8 1.7 %collective-permute-start.4 = (bf16[512,512]{1,0:T(8,128)(2,1)S(1)}, bf16[512,512]{1,0:T(8,128)(2,1)S(1)}, u32[]{:S(2)}, u32[]{:S(2)}) collective-permute-start(bf16[512,512]{1,0:T(8,128)(2,1)S(1)} %get-tuple-element.70), channel_id=1, source_target_pairs={{0,8},{1,9},{2,10},{3,11},{4,12},{5,13},{6,14},{7,15},{8,16},{9,17... | collective-permute-start | bytes 1572872 | tf_op jit(solution)/shard_map/ppermute | solution.py:40
  51.2 3.2 %collective-permute-start.13 = (bf16[512,512]{1,0:T(8,128)(2,1)S(1)}, bf16[512,512]{1,0:T(8,128)(2,1)S(1)}, u32[]{:S(2)}, u32[]{:S(2)}) collective-permute-start(bf16[512,512]{1,0:T(8,128)(2,1)S(1)} %get-tuple-element.86), channel_id=1, source_target_pairs={{0,3},{1,0},{2,1},{3,2},{4,7},{5,4},{6,5},{7,6},{8,11},{9,8},{10,9... | collective-permute-start | bytes 1572872 | tf_op jit(solution)/shard_map/ppermute | solution.py:40
  54.8 6.5 %collective-permute-done.10.refs_1_ = bf16[512,512]{1,0:T(8,128)(2,1)S(1)} collective-permute-done((bf16[512,512]{1,0:T(8,128)(2,1)S(1)}, bf16[512,512]{1,0:T(8,128)(2,1)S(1)}, u32[]{:S(2)}, u32[]{:S(2)}) %collective-permute-start.10) | collective-permute-done | bytes 524320 | tf_op jit(solution)/shard_map/ppermute | solution.py:40
  63.5 1.8 %collective-permute-start.8 = (bf16[512,512]{1,0:T(8,128)(2,1)S(1)}, bf16[512,512]{1,0:T(8,128)(2,1)S(1)}, u32[]{:S(2)}, u32[]{:S(2)}) collective-permute-start(bf16[512,512]{1,0:T(8,128)(2,1)S(1)} %sum_terms.11), channel_id=1, source_target_pairs={{0,24},{1,25},{2,26},{3,27},{4,28},{5,29},{6,30},{7,31},{8,0},{9,1... | collective-permute-start | bytes 1572872 | tf_op jit(solution)/shard_map/ppermute | solution.py:40
  65.4 1.8 %grad_own.1 = (bf16[512,512]{1,0:T(8,128)(2,1)S(1)}, bf16[512,512]{1,0:T(8,128)(2,1)S(1)}, bf16[512,512]{1,0:T(8,128)(2,1)S(1)}, bf16[512,512]{1,0:T(8,128)(2,1)S(1)}) custom-call(s32[3]{0:T(128)S(1)} %pad_add_fusion.pos_ref, bf16[512,8192]{1,0:T(8,128)(2,1)S(1)} %get-tuple-element.63.tokv_ref, bf16[512,512]{1,0:T(8,128)(2,1)S(1)} %get-tuple-element.65.cots_ref), custom_call_target="tpu_custom_call" | custom-call | flops 1073741824 | bytes 4194304 | tf_op jit(solution)/shard_map/grad_own/pallas_call | solution.py:116
  68.2 3.3 %collective-permute-start.14 = (bf16[512,512]{1,0:T(8,128)(2,1)S(1)}, bf16[512,512]{1,0:T(8,128)(2,1)}, u32[]{:S(2)}, u32[]{:S(2)}) collective-permute-start(bf16[512,512]{1,0:T(8,128)(2,1)S(1)} %sum_terms.14), channel_id=1, source_target_pairs={{0,3},{1,0},{2,1},{3,2},{4,7},{5,4},{6,5},{7,6},{8,11},{9,8},{10,9... | collective-permute-start | bytes 1572872 | tf_op jit(solution)/shard_map/ppermute | solution.py:40
  71.5 4.2 %collective-permute-done.11.refs_1_ = bf16[512,512]{1,0:T(8,128)(2,1)S(1)} collective-permute-done((bf16[512,512]{1,0:T(8,128)(2,1)S(1)}, bf16[512,512]{1,0:T(8,128)(2,1)S(1)}, u32[]{:S(2)}, u32[]{:S(2)}) %collective-permute-start.11) | collective-permute-done | bytes 524320 | tf_op jit(solution)/shard_map/ppermute | solution.py:40
  79.9 2.0 %collective-permute-start.22 = (bf16[512,512]{1,0:T(8,128)(2,1)S(1)}, bf16[512,512]{1,0:T(8,128)(2,1)S(1)}, u32[]{:S(2)}, u32[]{:S(2)}) collective-permute-start(bf16[512,512]{1,0:T(8,128)(2,1)S(1)} %get-tuple-element.103), channel_id=1, source_target_pairs={{0,24},{1,25},{2,26},{3,27},{4,28},{5,29},{6,30},{7,31},{8,0},{9,1... | collective-permute-start | bytes 1572872 | tf_op jit(solution)/shard_map/ppermute | solution.py:40
  83.0 3.4 %copy-done.1 = bf16[512,8192]{1,0:T(8,128)(2,1)S(1)} copy-done((bf16[512,8192]{1,0:T(8,128)(2,1)S(1)}, bf16[512,8192]{1,0:T(8,128)(2,1)}, u32[]{:S(2)}) %copy-start.1) | copy-done | bytes 8388632
  86.3 3.5 %gradh_own.1 = (bf16[512,2048]{1,0:T(8,128)(2,1)S(1)}, f32[512,128]{1,0:T(8,128)S(1)}) custom-call(s32[3]{0:T(128)S(1)} %pad_add_fusion.pos_ref, bf16[512,512]{1,0:T(8,128)(2,1)S(1)} %bitcast.23, bf16[512,8192]{1,0:T(8,128)(2,1)S(1)} %copy-done.1, bf16[1024,512]{1,0:T(8,128)(2,1)} %bitcast.29, bf16[512,512]{1,0:T(8,128)(2,1)} %copy-done.5, ...), custom_call_target="tpu_custom_call" | custom-call | flops 1073741824 | bytes 4194304 | tf_op jit(solution)/shard_map/gradh_own/pallas_call | solution.py:166
  89.9 3.0 %collective-permute-start.17 = (bf16[256,512]{1,0:T(8,128)(2,1)S(1)}, bf16[256,512]{1,0:T(8,128)(2,1)S(1)}, u32[]{:S(2)}, u32[]{:S(2)}) collective-permute-start(bf16[256,512]{1,0:T(8,128)(2,1)S(1)} %sum_terms.16), channel_id=1, source_target_pairs={{0,64},{64,0},{32,96},{96,32},{1,65},{65,1},{33,97},{97,33},{2,66}... | collective-permute-start | bytes 786440 | tf_op jit(solution)/shard_map/ppermute | solution.py:317
  92.9 3.1 %collective-permute-start.19 = (bf16[512,512]{1,0:T(8,128)(2,1)S(1)}, bf16[512,512]{1,0:T(8,128)(2,1)S(1)}, u32[]{:S(2)}, u32[]{:S(2)}) collective-permute-start(bf16[512,512]{1,0:T(8,128)(2,1)S(1)} %copy-done.6), channel_id=1, source_target_pairs={{0,3},{1,0},{2,1},{3,2},{4,7},{5,4},{6,5},{7,6},{8,11},{9,8},{10,9... | collective-permute-start | bytes 1572872 | tf_op jit(solution)/shard_map/ppermute | solution.py:40
  97.2 4.0 %collective-permute-done.17 = bf16[256,512]{1,0:T(8,128)(2,1)S(1)} collective-permute-done((bf16[256,512]{1,0:T(8,128)(2,1)S(1)}, bf16[256,512]{1,0:T(8,128)(2,1)S(1)}, u32[]{:S(2)}, u32[]{:S(2)}) %collective-permute-start.17) | collective-permute-done | bytes 262176 | tf_op jit(solution)/shard_map/ppermute | solution.py:317
  102.3 2.5 %collective-permute-start.30 = (bf16[512,512]{1,0:T(8,128)(2,1)S(1)}, bf16[512,512]{1,0:T(8,128)(2,1)S(1)}, u32[]{:S(2)}, u32[]{:S(2)}) collective-permute-start(bf16[512,512]{1,0:T(8,128)(2,1)S(1)} %get-tuple-element.112), channel_id=1, source_target_pairs={{0,24},{1,25},{2,26},{3,27},{4,28},{5,29},{6,30},{7,31},{8,0},{9,1... | collective-permute-start | bytes 1572872 | tf_op jit(solution)/shard_map/ppermute | solution.py:40
  104.8 5.4 %collective-permute-done.19.rest_3_ = bf16[512,512]{1,0:T(8,128)(2,1)S(1)} collective-permute-done((bf16[512,512]{1,0:T(8,128)(2,1)S(1)}, bf16[512,512]{1,0:T(8,128)(2,1)S(1)}, u32[]{:S(2)}, u32[]{:S(2)}) %collective-permute-start.19) | collective-permute-done | bytes 524320 | tf_op jit(solution)/shard_map/ppermute | solution.py:40
  110.2 3.8 %collective-permute-start.20 = (bf16[512,512]{1,0:T(8,128)(2,1)}, bf16[512,512]{1,0:T(8,128)(2,1)S(1)}, u32[]{:S(2)}, u32[]{:S(2)}) collective-permute-start(bf16[512,512]{1,0:T(8,128)(2,1)} %collective-permute-done.15.rest_2_), channel_id=1, source_target_pairs={{0,3},{1,0},{2,1},{3,2},{4,7},{5,4},{6,5},{7,6},{8,11},{9,8},{10,9... | collective-permute-start | bytes 1572872 | tf_op jit(solution)/shard_map/ppermute | solution.py:40
  114.0 1.8 %collective-permute-done.18.refs_3_ = bf16[512,512]{1,0:T(8,128)(2,1)S(1)} collective-permute-done((bf16[512,512]{1,0:T(8,128)(2,1)S(1)}, bf16[512,512]{1,0:T(8,128)(2,1)S(1)}, u32[]{:S(2)}, u32[]{:S(2)}) %collective-permute-start.18) | collective-permute-done | bytes 524320 | tf_op jit(solution)/shard_map/ppermute | solution.py:40
  116.9 2.9 %collective-permute-start.25 = (bf16[512,512]{1,0:T(8,128)(2,1)S(1)}, bf16[512,512]{1,0:T(8,128)(2,1)S(1)}, u32[]{:S(2)}, u32[]{:S(2)}) collective-permute-start(bf16[512,512]{1,0:T(8,128)(2,1)S(1)} %collective-permute-done.22.rest_1_), channel_id=1, source_target_pairs={{0,24},{1,25},{2,26},{3,27},{4,28},{5,29},{6,30},{7,31},{8,0},{9,1... | collective-permute-start | bytes 1572872 | tf_op jit(solution)/shard_map/ppermute | solution.py:40
  119.8 2.0 %collective-permute-start.33 = (bf16[512,512]{1,0:T(8,128)(2,1)S(1)}, bf16[512,512]{1,0:T(8,128)(2,1)S(1)}, u32[]{:S(2)}, u32[]{:S(2)}) collective-permute-start(bf16[512,512]{1,0:T(8,128)(2,1)S(1)} %collective-permute-done.19.rest_3_), channel_id=1, source_target_pairs={{0,3},{1,0},{2,1},{3,2},{4,7},{5,4},{6,5},{7,6},{8,11},{9,8},{10,9... | collective-permute-start | bytes 1572872 | tf_op jit(solution)/shard_map/ppermute | solution.py:40
  123.8 3.5 %gradh_one.1 = (bf16[512,2048]{1,0:T(8,128)(2,1)S(1)}, f32[512,128]{1,0:T(8,128)S(1)}) custom-call(s32[3]{0:T(128)S(1)} %pad_add_fusion.pos_ref, bf16[512,512]{1,0:T(8,128)(2,1)S(1)} %bitcast.24, bf16[512,8192]{1,0:T(8,128)(2,1)S(1)} %copy-done.1, bf16[512,512]{1,0:T(8,128)(2,1)} %copy-done.17, bf16[512,512]{1,0:T(8,128)(2,1)} %copy-done.16, ...), custom_call_target="tpu_custom_call" | custom-call | flops 1073741824 | bytes 4194304 | tf_op jit(solution)/shard_map/gradh_one/pallas_call | solution.py:166
  128.4 3.5 %gradh_two.1 = (bf16[512,2048]{1,0:T(8,128)(2,1)S(1)}, f32[512,128]{1,0:T(8,128)S(1)}) custom-call(s32[3]{0:T(128)S(1)} %pad_add_fusion.pos_ref, bf16[512,512]{1,0:T(8,128)(2,1)S(1)} %bitcast.25, bf16[512,8192]{1,0:T(8,128)(2,1)S(1)} %copy-done.1, bf16[512,512]{1,0:T(8,128)(2,1)} %copy-done.20, bf16[512,512]{1,0:T(8,128)(2,1)} %copy-done.21, ...), custom_call_target="tpu_custom_call" | custom-call | flops 1073741824 | bytes 4194304 | tf_op jit(solution)/shard_map/gradh_two/pallas_call | solution.py:166
  132.0 2.8 %collective-permute-start.28 = (bf16[128,512]{1,0:T(8,128)(2,1)S(1)}, bf16[128,512]{1,0:T(8,128)(2,1)S(1)}, u32[]{:S(2)}, u32[]{:S(2)}) collective-permute-start(bf16[128,512]{1,0:T(8,128)(2,1)S(1)} %get-tuple-element.108), channel_id=1, source_target_pairs={{0,24},{1,25},{2,26},{3,27},{4,28},{5,29},{6,30},{7,31},{8,0},{9,1... | collective-permute-start | bytes 393224 | tf_op jit(solution)/shard_map/ppermute | solution.py:40
  134.9 8.7 %input_gradient.1 = bf16[512,8192]{1,0:T(8,128)(2,1)} custom-call(s32[3]{0:T(128)S(1)} %pad_add_fusion.pos_ref, f32[512,128]{1,0:T(8,128)S(1)} %copy-done.12, bf16[512,512]{1,0:T(8,128)(2,1)S(1)} %bitcast.26, bf16[512,8192]{1,0:T(8,128)(2,1)S(1)} %copy-done.1, f32[512,128]{1,0:T(8,128)S(1)} %get-tuple-element.91.rest_0_, ...), custom_call_target="tpu_custom_call" | custom-call | flops 2147483648 | bytes 25165824 | tf_op jit(solution)/shard_map/input_gradient/pallas_call | solution.py:242
  (119 shorter events, 26.3 us)
Async XLA Ops:
  7.2 70.0 %all-gather.3.cloned.1.call-start = ((), (), s32[]{:S(2)}) async-start(), calls=%async_computation.2 | async-start | bytes 1179648 | tf_op jit(solution)/shard_map/all_gather | solution.py:339
  8.9 134.9 %reduce-scatter.2.cloned.1.call-start = ((), (), s32[]{:S(2)}) async-start(), calls=%async_computation.1 | async-start | bytes 1179648 | tf_op jit(solution)/shard_map/reduce_scatter | solution.py:399
  8.9 13.0 %collective-permute-start = (bf16[128,512]{1,0:T(8,128)(2,1)S(1)}, bf16[128,512]{1,0:T(8,128)(2,1)S(1)}, u32[]{:S(2)}, u32[]{:S(2)}) collective-permute-start(bf16[128,512]{1,0:T(8,128)(2,1)S(1)} %get-tuple-element.128.refs_0_), channel_id=1, source_target_pairs={{0,24},{1,25},{2,26},{3,27},{4,28},{5,29},{6,30},{7,31},{8,0},{9,1... | collective-permute-start | bytes 393224 | tf_op jit(solution)/shard_map/ppermute | solution.py:40
  23.8 22.9 %collective-permute-start.9 = (bf16[512,512]{1,0:T(8,128)(2,1)S(1)}, bf16[512,512]{1,0:T(8,128)(2,1)S(1)}, u32[]{:S(2)}, u32[]{:S(2)}) collective-permute-start(bf16[512,512]{1,0:T(8,128)(2,1)S(1)} %get-tuple-element.80), channel_id=1, source_target_pairs={{0,1},{1,2},{2,3},{3,0},{4,5},{5,6},{6,7},{7,4},{8,9},{9,10},{10,1... | collective-permute-start | bytes 1572872 | tf_op jit(solution)/shard_map/ppermute | solution.py:40
  25.8 20.9 %collective-permute-start.3 = (bf16[512,512]{1,0:T(8,128)(2,1)S(1)}, bf16[512,512]{1,0:T(8,128)(2,1)S(1)}, u32[]{:S(2)}, u32[]{:S(2)}) collective-permute-start(bf16[512,512]{1,0:T(8,128)(2,1)S(1)} %get-tuple-element.68), channel_id=1, source_target_pairs={{0,8},{1,9},{2,10},{3,11},{4,12},{5,13},{6,14},{7,15},{8,16},{9,17... | collective-permute-start | bytes 1572872 | tf_op jit(solution)/shard_map/ppermute | solution.py:40
  27.6 20.8 %collective-permute-start.6 = (bf16[512,512]{1,0:T(8,128)(2,1)S(1)}, bf16[512,512]{1,0:T(8,128)(2,1)S(1)}, u32[]{:S(2)}, u32[]{:S(2)}) collective-permute-start(bf16[512,512]{1,0:T(8,128)(2,1)S(1)} %get-tuple-element.73), channel_id=1, source_target_pairs={{0,24},{1,25},{2,26},{3,27},{4,28},{5,29},{6,30},{7,31},{8,0},{9,1... | collective-permute-start | bytes 1572872 | tf_op jit(solution)/shard_map/ppermute | solution.py:40
  29.1 22.1 %collective-permute-start.12 = (bf16[512,512]{1,0:T(8,128)(2,1)S(1)}, bf16[512,512]{1,0:T(8,128)(2,1)S(1)}, u32[]{:S(2)}, u32[]{:S(2)}) collective-permute-start(bf16[512,512]{1,0:T(8,128)(2,1)S(1)} %get-tuple-element.85), channel_id=1, source_target_pairs={{0,3},{1,0},{2,1},{3,2},{4,7},{5,4},{6,5},{7,6},{8,11},{9,8},{10,9... | collective-permute-start | bytes 1572872 | tf_op jit(solution)/shard_map/ppermute | solution.py:40
  46.7 14.5 %collective-permute-start.10 = (bf16[512,512]{1,0:T(8,128)(2,1)S(1)}, bf16[512,512]{1,0:T(8,128)(2,1)S(1)}, u32[]{:S(2)}, u32[]{:S(2)}) collective-permute-start(bf16[512,512]{1,0:T(8,128)(2,1)S(1)} %get-tuple-element.82), channel_id=1, source_target_pairs={{0,1},{1,2},{2,3},{3,0},{4,5},{5,6},{6,7},{7,4},{8,9},{9,10},{10,1... | collective-permute-start | bytes 1572872 | tf_op jit(solution)/shard_map/ppermute | solution.py:40
  46.8 15.3 %collective-permute-start.4 = (bf16[512,512]{1,0:T(8,128)(2,1)S(1)}, bf16[512,512]{1,0:T(8,128)(2,1)S(1)}, u32[]{:S(2)}, u32[]{:S(2)}) collective-permute-start(bf16[512,512]{1,0:T(8,128)(2,1)S(1)} %get-tuple-element.70), channel_id=1, source_target_pairs={{0,8},{1,9},{2,10},{3,11},{4,12},{5,13},{6,14},{7,15},{8,16},{9,17... | collective-permute-start | bytes 1572872 | tf_op jit(solution)/shard_map/ppermute | solution.py:40
  48.4 15.1 %collective-permute-start.7 = (bf16[512,512]{1,0:T(8,128)(2,1)S(1)}, bf16[512,512]{1,0:T(8,128)(2,1)S(1)}, u32[]{:S(2)}, u32[]{:S(2)}) collective-permute-start(bf16[512,512]{1,0:T(8,128)(2,1)S(1)} %get-tuple-element.74), channel_id=1, source_target_pairs={{0,24},{1,25},{2,26},{3,27},{4,28},{5,29},{6,30},{7,31},{8,0},{9,1... | collective-permute-start | bytes 1572872 | tf_op jit(solution)/shard_map/ppermute | solution.py:40
  50.0 18.0 %collective-permute-start.15 = (bf16[512,512]{1,0:T(8,128)(2,1)S(1)}, bf16[512,512]{1,0:T(8,128)(2,1)}, u32[]{:S(2)}, u32[]{:S(2)}) collective-permute-start(bf16[512,512]{1,0:T(8,128)(2,1)S(1)} %sum_terms.9.rest_1_), channel_id=1, source_target_pairs={{0,4},{1,5},{2,6},{3,7},{4,0},{5,1},{6,2},{7,3},{8,12},{9,13},{10,... | collective-permute-start | bytes 1572872 | tf_op jit(solution)/shard_map/ppermute | solution.py:40
  51.2 17.0 %collective-permute-start.13 = (bf16[512,512]{1,0:T(8,128)(2,1)S(1)}, bf16[512,512]{1,0:T(8,128)(2,1)S(1)}, u32[]{:S(2)}, u32[]{:S(2)}) collective-permute-start(bf16[512,512]{1,0:T(8,128)(2,1)S(1)} %get-tuple-element.86), channel_id=1, source_target_pairs={{0,3},{1,0},{2,1},{3,2},{4,7},{5,4},{6,5},{7,6},{8,11},{9,8},{10,9... | collective-permute-start | bytes 1572872 | tf_op jit(solution)/shard_map/ppermute | solution.py:40
  62.1 13.6 %collective-permute-start.11 = (bf16[512,512]{1,0:T(8,128)(2,1)S(1)}, bf16[512,512]{1,0:T(8,128)(2,1)S(1)}, u32[]{:S(2)}, u32[]{:S(2)}) collective-permute-start(bf16[512,512]{1,0:T(8,128)(2,1)S(1)} %sum_terms.13), channel_id=1, source_target_pairs={{0,1},{1,2},{2,3},{3,0},{4,5},{5,6},{6,7},{7,4},{8,9},{9,10},{10,1... | collective-permute-start | bytes 1572872 | tf_op jit(solution)/shard_map/ppermute | solution.py:40
  62.1 13.6 %collective-permute-start.5 = (bf16[512,512]{1,0:T(8,128)(2,1)S(1)}, bf16[512,512]{1,0:T(8,128)(2,1)S(1)}, u32[]{:S(2)}, u32[]{:S(2)}) collective-permute-start(bf16[512,512]{1,0:T(8,128)(2,1)S(1)} %sum_terms.10), channel_id=1, source_target_pairs={{0,8},{1,9},{2,10},{3,11},{4,12},{5,13},{6,14},{7,15},{8,16},{9,17... | collective-permute-start | bytes 1572872 | tf_op jit(solution)/shard_map/ppermute | solution.py:40
  63.5 12.2 %collective-permute-start.8 = (bf16[512,512]{1,0:T(8,128)(2,1)S(1)}, bf16[512,512]{1,0:T(8,128)(2,1)S(1)}, u32[]{:S(2)}, u32[]{:S(2)}) collective-permute-start(bf16[512,512]{1,0:T(8,128)(2,1)S(1)} %sum_terms.11), channel_id=1, source_target_pairs={{0,24},{1,25},{2,26},{3,27},{4,28},{5,29},{6,30},{7,31},{8,0},{9,1... | collective-permute-start | bytes 1572872 | tf_op jit(solution)/shard_map/ppermute | solution.py:40
  68.0 13.9 %collective-permute-start.16 = (bf16[256,512]{1,0:T(8,128)(2,1)S(1)}, bf16[256,512]{1,0:T(8,128)(2,1)}, u32[]{:S(2)}, u32[]{:S(2)}) collective-permute-start(bf16[256,512]{1,0:T(8,128)(2,1)S(1)} %convert_bitcast_fusion.refs_0_), channel_id=1, source_target_pairs={{0,32},{32,0},{64,96},{96,64},{1,33},{33,1},{65,97},{97,65},{2,34}... | collective-permute-start | bytes 786440 | tf_op jit(solution)/shard_map/ppermute | solution.py:317
  68.2 24.7 %collective-permute-start.14 = (bf16[512,512]{1,0:T(8,128)(2,1)S(1)}, bf16[512,512]{1,0:T(8,128)(2,1)}, u32[]{:S(2)}, u32[]{:S(2)}) collective-permute-start(bf16[512,512]{1,0:T(8,128)(2,1)S(1)} %sum_terms.14), channel_id=1, source_target_pairs={{0,3},{1,0},{2,1},{3,2},{4,7},{5,4},{6,5},{7,6},{8,11},{9,8},{10,9... | collective-permute-start | bytes 1572872 | tf_op jit(solution)/shard_map/ppermute | solution.py:40
  75.7 25.8 %collective-permute-start.29 = (bf16[512,512]{1,0:T(8,128)(2,1)}, bf16[512,512]{1,0:T(8,128)(2,1)}, u32[]{:S(2)}, u32[]{:S(2)}) collective-permute-start(bf16[512,512]{1,0:T(8,128)(2,1)} %collective-permute-done.15.rest_2_), channel_id=1, source_target_pairs={{0,1},{1,2},{2,3},{3,0},{4,5},{5,6},{6,7},{7,4},{8,9},{9,10},{10,1... | collective-permute-start | bytes 1572872 | tf_op jit(solution)/shard_map/ppermute | solution.py:40
  78.6 22.8 %collective-permute-start.23 = (bf16[512,512]{1,0:T(8,128)(2,1)S(1)}, bf16[512,512]{1,0:T(8,128)(2,1)S(1)}, u32[]{:S(2)}, u32[]{:S(2)}) collective-permute-start(bf16[512,512]{1,0:T(8,128)(2,1)S(1)} %get-tuple-element.112), channel_id=1, source_target_pairs={{0,8},{1,9},{2,10},{3,11},{4,12},{5,13},{6,14},{7,15},{8,16},{9,17... | collective-permute-start | bytes 1572872 | tf_op jit(solution)/shard_map/ppermute | solution.py:40
  79.9 22.4 %collective-permute-start.22 = (bf16[512,512]{1,0:T(8,128)(2,1)S(1)}, bf16[512,512]{1,0:T(8,128)(2,1)S(1)}, u32[]{:S(2)}, u32[]{:S(2)}) collective-permute-start(bf16[512,512]{1,0:T(8,128)(2,1)S(1)} %get-tuple-element.103), channel_id=1, source_target_pairs={{0,24},{1,25},{2,26},{3,27},{4,28},{5,29},{6,30},{7,31},{8,0},{9,1... | collective-permute-start | bytes 1572872 | tf_op jit(solution)/shard_map/ppermute | solution.py:40
  92.9 17.3 %collective-permute-start.19 = (bf16[512,512]{1,0:T(8,128)(2,1)S(1)}, bf16[512,512]{1,0:T(8,128)(2,1)S(1)}, u32[]{:S(2)}, u32[]{:S(2)}) collective-permute-start(bf16[512,512]{1,0:T(8,128)(2,1)S(1)} %copy-done.6), channel_id=1, source_target_pairs={{0,3},{1,0},{2,1},{3,2},{4,7},{5,4},{6,5},{7,6},{8,11},{9,8},{10,9... | collective-permute-start | bytes 1572872 | tf_op jit(solution)/shard_map/ppermute | solution.py:40
  101.2 14.6 %collective-permute-start.18 = (bf16[512,512]{1,0:T(8,128)(2,1)S(1)}, bf16[512,512]{1,0:T(8,128)(2,1)S(1)}, u32[]{:S(2)}, u32[]{:S(2)}) collective-permute-start(bf16[512,512]{1,0:T(8,128)(2,1)S(1)} %sum_terms.15), channel_id=1, source_target_pairs={{0,4},{1,5},{2,6},{3,7},{4,0},{5,1},{6,2},{7,3},{8,12},{9,13},{10,... | collective-permute-start | bytes 1572872 | tf_op jit(solution)/shard_map/ppermute | solution.py:40
  101.5 15.4 %collective-permute-start.31 = (bf16[512,512]{1,0:T(8,128)(2,1)S(1)}, bf16[512,512]{1,0:T(8,128)(2,1)S(1)}, u32[]{:S(2)}, u32[]{:S(2)}) collective-permute-start(bf16[512,512]{1,0:T(8,128)(2,1)S(1)} %copy-done.6), channel_id=1, source_target_pairs={{0,1},{1,2},{2,3},{3,0},{4,5},{5,6},{6,7},{7,4},{8,9},{9,10},{10,1... | collective-permute-start | bytes 1572872 | tf_op jit(solution)/shard_map/ppermute | solution.py:40
  101.5 15.4 %collective-permute-start.24 = (bf16[512,512]{1,0:T(8,128)(2,1)S(1)}, bf16[512,512]{1,0:T(8,128)(2,1)S(1)}, u32[]{:S(2)}, u32[]{:S(2)}) collective-permute-start(bf16[512,512]{1,0:T(8,128)(2,1)S(1)} %get-tuple-element.103), channel_id=1, source_target_pairs={{0,8},{1,9},{2,10},{3,11},{4,12},{5,13},{6,14},{7,15},{8,16},{9,17... | collective-permute-start | bytes 1572872 | tf_op jit(solution)/shard_map/ppermute | solution.py:40
  102.3 19.5 %collective-permute-start.30 = (bf16[512,512]{1,0:T(8,128)(2,1)S(1)}, bf16[512,512]{1,0:T(8,128)(2,1)S(1)}, u32[]{:S(2)}, u32[]{:S(2)}) collective-permute-start(bf16[512,512]{1,0:T(8,128)(2,1)S(1)} %get-tuple-element.112), channel_id=1, source_target_pairs={{0,24},{1,25},{2,26},{3,27},{4,28},{5,29},{6,30},{7,31},{8,0},{9,1... | collective-permute-start | bytes 1572872 | tf_op jit(solution)/shard_map/ppermute | solution.py:40
  110.2 17.4 %collective-permute-start.20 = (bf16[512,512]{1,0:T(8,128)(2,1)}, bf16[512,512]{1,0:T(8,128)(2,1)S(1)}, u32[]{:S(2)}, u32[]{:S(2)}) collective-permute-start(bf16[512,512]{1,0:T(8,128)(2,1)} %collective-permute-done.15.rest_2_), channel_id=1, source_target_pairs={{0,3},{1,0},{2,1},{3,2},{4,7},{5,4},{6,5},{7,6},{8,11},{9,8},{10,9... | collective-permute-start | bytes 1572872 | tf_op jit(solution)/shard_map/ppermute | solution.py:40
  115.8 16.2 %collective-permute-start.27 = (bf16[512,512]{1,0:T(8,128)(2,1)S(1)}, bf16[512,512]{1,0:T(8,128)(2,1)S(1)}, u32[]{:S(2)}, u32[]{:S(2)}) collective-permute-start(bf16[512,512]{1,0:T(8,128)(2,1)S(1)} %collective-permute-done.23.rest_0_), channel_id=1, source_target_pairs={{0,8},{1,9},{2,10},{3,11},{4,12},{5,13},{6,14},{7,15},{8,16},{9,17... | collective-permute-start | bytes 1572872 | tf_op jit(solution)/shard_map/ppermute | solution.py:40
  116.9 18.0 %collective-permute-start.25 = (bf16[512,512]{1,0:T(8,128)(2,1)S(1)}, bf16[512,512]{1,0:T(8,128)(2,1)S(1)}, u32[]{:S(2)}, u32[]{:S(2)}) collective-permute-start(bf16[512,512]{1,0:T(8,128)(2,1)S(1)} %collective-permute-done.22.rest_1_), channel_id=1, source_target_pairs={{0,24},{1,25},{2,26},{3,27},{4,28},{5,29},{6,30},{7,31},{8,0},{9,1... | collective-permute-start | bytes 1572872 | tf_op jit(solution)/shard_map/ppermute | solution.py:40
  119.8 15.0 %collective-permute-start.33 = (bf16[512,512]{1,0:T(8,128)(2,1)S(1)}, bf16[512,512]{1,0:T(8,128)(2,1)S(1)}, u32[]{:S(2)}, u32[]{:S(2)}) collective-permute-start(bf16[512,512]{1,0:T(8,128)(2,1)S(1)} %collective-permute-done.19.rest_3_), channel_id=1, source_target_pairs={{0,3},{1,0},{2,1},{3,2},{4,7},{5,4},{6,5},{7,6},{8,11},{9,8},{10,9... | collective-permute-start | bytes 1572872 | tf_op jit(solution)/shard_map/ppermute | solution.py:40
  121.8 13.1 %collective-permute-start.32 = (bf16[512,512]{1,0:T(8,128)(2,1)}, bf16[512,512]{1,0:T(8,128)(2,1)S(1)}, u32[]{:S(2)}, u32[]{:S(2)}) collective-permute-start(bf16[512,512]{1,0:T(8,128)(2,1)} %collective-permute-done.29.rest_2_), channel_id=1, source_target_pairs={{0,1},{1,2},{2,3},{3,0},{4,5},{5,6},{6,7},{7,4},{8,9},{9,10},{10,1... | collective-permute-start | bytes 1572872 | tf_op jit(solution)/shard_map/ppermute | solution.py:40
  127.7 16.0 %collective-permute-start.21 = (bf16[128,512]{1,0:T(8,128)(2,1)S(1)}, bf16[128,512]{1,0:T(8,128)(2,1)S(1)}, u32[]{:S(2)}, u32[]{:S(2)}) collective-permute-start(bf16[128,512]{1,0:T(8,128)(2,1)S(1)} %get-tuple-element.99), channel_id=1, source_target_pairs={{0,8},{1,9},{2,10},{3,11},{4,12},{5,13},{6,14},{7,15},{8,16},{9,17... | collective-permute-start | bytes 393224 | tf_op jit(solution)/shard_map/ppermute | solution.py:40
  132.0 11.6 %collective-permute-start.28 = (bf16[128,512]{1,0:T(8,128)(2,1)S(1)}, bf16[128,512]{1,0:T(8,128)(2,1)S(1)}, u32[]{:S(2)}, u32[]{:S(2)}) collective-permute-start(bf16[128,512]{1,0:T(8,128)(2,1)S(1)} %get-tuple-element.108), channel_id=1, source_target_pairs={{0,24},{1,25},{2,26},{3,27},{4,28},{5,29},{6,30},{7,31},{8,0},{9,1... | collective-permute-start | bytes 393224 | tf_op jit(solution)/shard_map/ppermute | solution.py:40
  (30 other events, 448.2 us)
Sparse Core Ops, SparseCore 0:
  10.2 41.6 all-gather.2
  77.2 42.2 reduce-scatter.1
